TPU v7x, 256 devices: a whole 4x4x8 slice. The times are simulated.
256 devices in a mesh: seq: 32 (over y, z_lo, core), fsdp: 8 (over x, z_hi).
Axes of the slice: x: 4, y: 4, z: 8 (z_hi: 2, z_lo: 4; z = z_hi * 4 + z_lo), core: 2. Of those that a mesh axis runs over, the one named last changes fastest.
Arguments:
- queries: bfloat16 [8, 16384, 1024], P('fsdp', 'seq'), may hold values from -10.5 to 10.5
- key_vectors: bfloat16 [8, 16384, 1024], P('fsdp', 'seq'), may hold values from -10.5 to 10.5
- value_vectors: bfloat16 [8, 16384, 1024], P('fsdp', 'seq'), may hold values from -6 to 6
- grad_mixed: bfloat16 [8, 16384, 2048], P('fsdp', 'seq'), may hold values from -24 to 24
- out_weight: bfloat16 [1024, 2048], P('fsdp'), may hold values from -0.1875 to 0.1875
- head_phase: int32 [8], replicated, may hold values from 0 to 3
- segments_short: int32 [15], replicated, may hold values from 1 to 2048, 16384 in all
- segments_long: int32 [3], replicated, may hold values from 1 to 8192, as said below
Outputs:
- grad_query: bfloat16 [8, 16384, 1024], P('fsdp', 'seq')
- grad_key: bfloat16 [8, 16384, 1024], P('fsdp', 'seq')
- grad_value: bfloat16 [8, 16384, 1024], P('fsdp', 'seq')
Inputs may be any that keep to these rules, and one draw needn't show every extreme that they name: `segments_long`: lengths that sum to 16384; the last of them is 8192, the others are shorter.
All inputs are finite; a program needn't handle non-finite values.
Results may differ from a plain program's by a relative error of at most 0.0095.
Values may be sent and summed in bfloat16 or wider, within the bound.
A program may use at most 256 MiB of HBM per device.

v0:
```python
import math

import jax
import jax.numpy as jnp
from jax import lax
from jax.sharding import PartitionSpec as P

REACH_SHORT = 4
REACH_LONG = 16


VERY_NEGATIVE = -1e30


def passed_along(value, axis, by):
    devices = lax.axis_size(axis)
    pairs = [(i, i + by) for i in range(devices) if 0 <= i + by < devices]
    return lax.ppermute(value, axis, pairs)


def take_half(tensor, parity):
    layout = tensor.shape
    paired = tensor.reshape(layout[:-3] + (layout[-3] // 2, 2) + layout[-2:])
    return jnp.where((parity == 0)[:, None], paired[..., 0, :, :], paired[..., 1, :, :])


def put_half(tensor, parity):
    zero_fill = jnp.zeros_like(tensor)
    first_half = jnp.where((parity == 0)[:, None], tensor, zero_fill)
    second_half = jnp.where((parity == 1)[:, None], tensor, zero_fill)
    stacked = jnp.stack([first_half, second_half], axis=-3)
    return stacked.reshape(tensor.shape[:-3] + (2 * tensor.shape[-3],) + tensor.shape[-2:])


def stat_half(tensor, parity):
    paired = tensor.reshape(tensor.shape[0], tensor.shape[1] // 2, 2)
    return jnp.where((parity == 0)[:, None], paired[:, :, 0], paired[:, :, 1])


def stat_put(tensor, parity, fill_value):
    filler = jnp.full_like(tensor, fill_value)
    first_half = jnp.where((parity == 0)[:, None], tensor, filler)
    second_half = jnp.where((parity == 1)[:, None], tensor, filler)
    return jnp.stack([first_half, second_half], axis=-1).reshape(
        tensor.shape[0], 2 * tensor.shape[1]
    )


def segment_of(positions, lengths):
    seg_ends = jnp.cumsum(lengths)
    return jnp.sum((positions[..., None] >= seg_ends).astype(jnp.int32), axis=-1)


def row_positions(shard_index, tok_dev, stride, offset, row_count):
    return (
        shard_index * tok_dev
        + stride * jnp.arange(row_count, dtype=jnp.int32)[None, :]
        + offset[:, None]
    )


def pair_mask(query_pos, key_pos, lengths):
    query_seg = segment_of(query_pos, lengths)
    key_seg = segment_of(key_pos, lengths)
    causal = key_pos[:, None, :] <= query_pos[:, :, None]
    same_seg = key_seg[:, None, :] == query_seg[:, :, None]
    return causal & same_seg & (key_pos[:, None, :] >= 0)


def product(pattern, left_operand, right_operand):
    return jnp.einsum(pattern, left_operand, right_operand, preferred_element_type=jnp.float32)


def guarded(is_live, compute, shapes):
    return compute()


def shard_grads(
    shard_index,
    query_rows,
    grad_rows,
    near_window,
    far_window,
    head_phase,
    segments_short,
    segments_long,
    guard_fn,
    product_fn,
):
    rows_short, head_count, head_width = query_rows.shape
    tok_dev = 2 * rows_short
    score_scale = 1.0 / math.sqrt(head_width)
    par_short = head_phase % 2
    par_long = head_phase // 2
    query_long = take_half(query_rows, par_long)
    grad_long = take_half(grad_rows, par_long)
    levels = [
        (query_rows, grad_rows, near_window, 2, par_short, segments_short),
        (query_long, grad_long, far_window, 4, head_phase, segments_long),
    ]
    stored = []
    peak_list = []
    for query_here, grad_here, window, stride, offset, lengths in levels:
        row_count = query_here.shape[0]
        query_pos = row_positions(shard_index, tok_dev, stride, offset, row_count)
        blocks = []
        top_here = jnp.full((head_count, row_count), VERY_NEGATIVE, jnp.float32)
        for distance in range(len(window)):
            key_pos = row_positions(shard_index - distance, tok_dev, stride, offset, row_count)
            live_pairs = pair_mask(query_pos, key_pos, lengths)

            def score_block(query_here=query_here, key_here=window[distance][0]):
                return (product_fn("qhd,khd->hqk", query_here, key_here) * score_scale,)

            raw_scores = guard_fn(
                jnp.any(live_pairs), score_block, ((head_count, row_count, row_count),)
            )[0]
            scores = jnp.where(live_pairs, raw_scores, VERY_NEGATIVE)
            top_here = jnp.maximum(top_here, jnp.max(scores, axis=-1))
            blocks.append((live_pairs, scores))
        stored.append(blocks)
        peak_list.append(top_here)
    top_short = jnp.maximum(peak_list[0], stat_put(peak_list[1], par_long, VERY_NEGATIVE))
    level_tops = [top_short, stat_half(top_short, par_long)]
    totals = []
    numerators = []
    for level_index, (query_here, grad_here, window, stride, offset, lengths) in enumerate(levels):
        row_count = query_here.shape[0]
        total_here = jnp.zeros((head_count, row_count), jnp.float32)
        numer_here = jnp.zeros((row_count, head_count, head_width), jnp.float32)
        for distance, (live_pairs, scores) in enumerate(stored[level_index]):
            weights = jnp.where(
                live_pairs, jnp.exp(scores - level_tops[level_index][:, :, None]), 0.0
            )
            total_here = total_here + jnp.sum(weights, axis=-1)

            def weight_block(weights=weights, value_here=window[distance][1]):
                return (product_fn("hqk,khd->qhd", weights.astype(jnp.bfloat16), value_here),)

            numer_here = (
                numer_here
                + guard_fn(
                    jnp.any(live_pairs), weight_block, ((row_count, head_count, head_width),)
                )[0]
            )
        totals.append(total_here)
        numerators.append(numer_here)
    denominator = totals[0] + stat_put(totals[1], par_long, 0.0)
    attended = (numerators[0] + put_half(numerators[1], par_long)) / jnp.transpose(denominator)[
        :, :, None
    ]
    delta_rows = jnp.transpose(jnp.sum(grad_rows.astype(jnp.float32) * attended, axis=-1))
    inverse = 1.0 / denominator
    level_inverse = [inverse, stat_half(inverse, par_long)]
    level_delta = [delta_rows, stat_half(delta_rows, par_long)]
    grad_levels = []
    part_levels = []
    for level_index, (query_here, grad_here, window, stride, offset, lengths) in enumerate(levels):
        row_count = query_here.shape[0]
        grad_sum = jnp.zeros((row_count, head_count, head_width), jnp.float32)
        part_list = []
        for distance, (live_pairs, scores) in enumerate(stored[level_index]):

            def backward_block(
                live_pairs=live_pairs,
                scores=scores,
                key_here=window[distance][0],
                value_here=window[distance][1],
                query_here=query_here,
                grad_here=grad_here,
                top_here=level_tops[level_index],
                inverse_here=level_inverse[level_index],
                delta_here=level_delta[level_index],
            ):
                probability = (
                    jnp.where(live_pairs, jnp.exp(scores - top_here[:, :, None]), 0.0)
                    * inverse_here[:, :, None]
                )
                grad_probs = product_fn("qhd,khd->hqk", grad_here, value_here)
                grad_scores = (probability * (grad_probs - delta_here[:, :, None])).astype(
                    jnp.bfloat16
                )
                return (
                    product_fn("hqk,khd->qhd", grad_scores, key_here) * score_scale,
                    product_fn("hqk,qhd->khd", grad_scores, query_here) * score_scale,
                    product_fn("hqk,qhd->khd", probability.astype(jnp.bfloat16), grad_here),
                )

            shapes = ((row_count, head_count, head_width),) * 3
            add_query, part_key, part_value = guard_fn(jnp.any(live_pairs), backward_block, shapes)
            grad_sum = grad_sum + add_query
            part_list.append((part_key, part_value))
        grad_levels.append(grad_sum)
        part_levels.append(part_list)
    grad_query = grad_levels[0] + put_half(grad_levels[1], par_long)
    near_parts = []
    for distance in range(len(near_window)):
        key_part = part_levels[0][distance][0] + put_half(part_levels[1][distance][0], par_long)
        value_part = part_levels[0][distance][1] + put_half(part_levels[1][distance][1], par_long)
        near_parts.append(jnp.stack([key_part, value_part]).astype(jnp.bfloat16))
    far_parts = [
        jnp.stack([part_levels[1][distance][0], part_levels[1][distance][1]]).astype(jnp.bfloat16)
        for distance in range(len(near_window), len(far_window))
    ]
    return (grad_query, near_parts, far_parts, (top_short, inverse, delta_rows))


def shards(
    queries,
    key_vectors,
    value_vectors,
    grad_mixed,
    out_weight,
    head_phase,
    segments_short,
    segments_long,
):
    shard_index = lax.axis_index("seq")
    tok_dev = queries.shape[1]
    head_count = head_phase.shape[0]
    head_width = queries.shape[2] // head_count
    par_short = head_phase % 2
    par_long = head_phase // 2
    grad_out = jnp.einsum(
        "td,rd->tr",
        grad_mixed[0],
        lax.all_gather(out_weight, "fsdp", axis=0, tiled=True),
        preferred_element_type=jnp.float32,
    ).astype(jnp.bfloat16)

    def split_rows(tensor):
        return take_half(tensor.reshape(tok_dev, head_count, head_width), par_short)

    query_rows = split_rows(queries[0])
    grad_rows = split_rows(grad_out)
    own_short = jnp.stack([split_rows(key_vectors[0]), split_rows(value_vectors[0])])
    own_long = take_half(own_short, par_long)
    near_window = [own_short]
    far_window = [own_long]
    for distance in range(1, REACH_SHORT + 1):
        arrived = passed_along(own_short, "seq", distance)
        near_window.append(arrived)
        far_window.append(take_half(arrived, par_long))
    for distance in range(REACH_SHORT + 1, REACH_LONG + 1):
        far_window.append(passed_along(own_long, "seq", distance))
    grad_query, near_parts, far_parts, row_stats = shard_grads(
        shard_index,
        query_rows,
        grad_rows,
        near_window,
        far_window,
        head_phase,
        segments_short,
        segments_long,
        guarded,
        product,
    )
    summed = near_parts[0].astype(jnp.float32)
    far_sum = jnp.zeros(own_long.shape, jnp.float32)
    for distance in range(1, REACH_SHORT + 1):
        summed = summed + passed_along(near_parts[distance], "seq", -distance).astype(jnp.float32)
    for distance in range(REACH_SHORT + 1, REACH_LONG + 1):
        far_sum = far_sum + passed_along(
            far_parts[distance - REACH_SHORT - 1], "seq", -distance
        ).astype(jnp.float32)
    summed = summed + put_half(far_sum, par_long)
    final_pair = summed.astype(jnp.bfloat16)

    def to_tokens(rows_here):
        return put_half(rows_here, par_short).reshape(1, tok_dev, head_count * head_width)

    return (
        to_tokens(grad_query.astype(jnp.bfloat16)),
        to_tokens(final_pair[0]),
        to_tokens(final_pair[1]),
    )


def solution(mesh):
    placed = (
        P("fsdp", "seq", None),
        P("fsdp", "seq", None),
        P("fsdp", "seq", None),
        P("fsdp", "seq", None),
        P("fsdp", None),
        P(),
        P(),
        P(),
    )
    return jax.shard_map(
        shards,
        mesh=mesh,
        in_specs=placed,
        out_specs=(P("fsdp", "seq", None), P("fsdp", "seq", None), P("fsdp", "seq", None)),
        check_vma=False,
    )
```

profile of v0, /device:TPU:107, one launch (start us, length us, event | category | flops | bytes accessed | tf_op | source)
XLA Modules:
  0.0 861.1 jit_solution(2770081277454938744)
XLA Ops:
  15.1 5.7 collective-permute-start.2
  22.8 3.4 collective-permute-start
  33.5 2.6 copy.1154
  37.5 113.3 %collective-permute-done = bf16[2,256,8,128]{3,1,2,0:T(8,128)(2,1)} collective-permute-done((bf16[2,256,8,128]{3,1,2,0:T(8,128)(2,1)}, bf16[2,256,8,128]{3,1,2,0:T(8,128)(2,1)}, u32[]{:S(2)}, u32[]{:S(2)}) %collective-permute-start) | collective-permute-done | bytes 1048608 | tf_op jit(solution)/shard_map/ppermute | solution.py:18
  150.8 3.6 fusion.323
  154.5 3.7 fusion.324
  158.2 3.6 fusion.325
  167.6 2.7 collective-permute-start.14
  170.2 22.7 %collective-permute-start.13 = (bf16[2,128,8,128]{3,1,2,0:T(8,128)(2,1)}, bf16[2,128,8,128]{3,1,2,0:T(8,128)(2,1)}, u32[]{:S(2)}, u32[]{:S(2)}) collective-permute-start(bf16[2,128,8,128]{3,1,2,0:T(8,128)(2,1)} %get-tuple-element.166), channel_id=1, source_target_pairs={{0,112},{8,120},{16,128},{24,136},{32,144},{40,152},{48,160},{56,1... | collective-permute-start | bytes 1572872 | tf_op jit(solution)/shard_map/ppermute | solution.py:18
  192.9 16.6 %collective-permute-start.12 = (bf16[2,128,8,128]{3,1,2,0:T(8,128)(2,1)}, bf16[2,128,8,128]{3,1,2,0:T(8,128)(2,1)}, u32[]{:S(2)}, u32[]{:S(2)}) collective-permute-start(bf16[2,128,8,128]{3,1,2,0:T(8,128)(2,1)} %get-tuple-element.166), channel_id=1, source_target_pairs={{0,104},{8,112},{16,120},{24,128},{32,136},{40,144},{48,152},{56,1... | collective-permute-start | bytes 1572872 | tf_op jit(solution)/shard_map/ppermute | solution.py:18
  211.6 4.6 fusion.10
  219.2 2.3 fusion.348
  233.0 2.3 fusion.333
  235.4 5.0 collective-permute-start.8
  242.7 11.2 %collective-permute-done.12 = bf16[2,128,8,128]{3,1,2,0:T(8,128)(2,1)} collective-permute-done((bf16[2,128,8,128]{3,1,2,0:T(8,128)(2,1)}, bf16[2,128,8,128]{3,1,2,0:T(8,128)(2,1)}, u32[]{:S(2)}, u32[]{:S(2)}) %collective-permute-start.12) | collective-permute-done | bytes 524320 | tf_op jit(solution)/shard_map/ppermute | solution.py:18
  258.1 9.9 %collective-permute-done.11 = bf16[2,128,8,128]{3,1,2,0:T(8,128)(2,1)} collective-permute-done((bf16[2,128,8,128]{3,1,2,0:T(8,128)(2,1)}, bf16[2,128,8,128]{3,1,2,0:T(8,128)(2,1)}, u32[]{:S(2)}, u32[]{:S(2)}) %collective-permute-start.11) | collective-permute-done | bytes 524320 | tf_op jit(solution)/shard_map/ppermute | solution.py:18
  272.2 34.8 %collective-permute-done.10 = bf16[2,128,8,128]{3,1,2,0:T(8,128)(2,1)S(1)} collective-permute-done((bf16[2,128,8,128]{3,1,2,0:T(8,128)(2,1)}, bf16[2,128,8,128]{3,1,2,0:T(8,128)(2,1)S(1)}, u32[]{:S(2)}, u32[]{:S(2)}) %collective-permute-start.10) | collective-permute-done | bytes 524320 | tf_op jit(solution)/shard_map/ppermute | solution.py:18
  310.3 3.1 collective-permute-done.9
  313.4 12.1 %collective-permute-start.4 = (bf16[2,128,8,128]{3,1,2,0:T(8,128)(2,1)}, bf16[2,128,8,128]{3,1,2,0:T(8,128)(2,1)S(1)}, u32[]{:S(2)}, u32[]{:S(2)}) collective-permute-start(bf16[2,128,8,128]{3,1,2,0:T(8,128)(2,1)} %get-tuple-element.166), channel_id=1, source_target_pairs={{0,40},{8,48},{16,56},{24,64},{32,72},{40,80},{48,88},{56,96},{64,... | collective-permute-start | bytes 1572872 | tf_op jit(solution)/shard_map/ppermute | solution.py:18
  330.2 27.5 %collective-permute-done.6 = bf16[2,128,8,128]{3,1,2,0:T(8,128)(2,1)S(1)} collective-permute-done((bf16[2,128,8,128]{3,1,2,0:T(8,128)(2,1)}, bf16[2,128,8,128]{3,1,2,0:T(8,128)(2,1)S(1)}, u32[]{:S(2)}, u32[]{:S(2)}) %collective-permute-start.6) | collective-permute-done | bytes 524320 | tf_op jit(solution)/shard_map/ppermute | solution.py:18
  359.7 21.0 %collective-permute-done.5 = bf16[2,128,8,128]{3,1,2,0:T(8,128)(2,1)S(1)} collective-permute-done((bf16[2,128,8,128]{3,1,2,0:T(8,128)(2,1)}, bf16[2,128,8,128]{3,1,2,0:T(8,128)(2,1)S(1)}, u32[]{:S(2)}, u32[]{:S(2)}) %collective-permute-start.5) | collective-permute-done | bytes 524320 | tf_op jit(solution)/shard_map/ppermute | solution.py:18
  384.7 7.1 collective-permute-done.4
  398.8 5.3 fusion.2
  404.1 2.9 fusion.3
  410.3 5.0 fusion.296
  415.4 5.1 fusion.299
  420.5 4.9 fusion.302
  427.1 2.3 fusion.293
  429.8 6.6 fusion.318
  437.2 2.7 fusion.252
  439.9 4.5 fusion.180
  452.7 2.4 fusion.233
  477.9 3.8 fusion.176
  481.7 3.1 fusion.174
  484.9 3.8 convolution_add_fusion.3
  488.7 3.3 fusion.50
  554.5 21.5 %collective-permute-start.20 = (bf16[2,128,8,128]{3,1,2,0:T(8,128)(2,1)S(1)}, bf16[2,128,8,128]{3,1,2,0:T(8,128)(2,1)S(1)}, u32[]{:S(2)}, u32[]{:S(2)}) collective-permute-start(bf16[2,128,8,128]{3,1,2,0:T(8,128)(2,1)S(1)} %pad_maximum_fusion.22), channel_id=1, source_target_pairs={{40,0},{48,8},{56,16},{64,24},{72,32},{80,40},{88,48},{96,56},{104... | collective-permute-start | bytes 1572872 | tf_op jit(solution)/shard_map/ppermute | solution.py:18
  578.1 3.6 collective-permute-start.29
  600.7 2.3 multiply_convert_fusion.3
  603.5 2.3 multiply_convert_fusion.2
  606.3 2.3 multiply_convert_fusion.1
  638.5 45.0 %collective-permute-done.27 = bf16[2,128,8,128]{3,1,2,0:T(8,128)(2,1)S(1)} collective-permute-done((bf16[2,128,8,128]{3,1,2,0:T(8,128)(2,1)S(1)}, bf16[2,128,8,128]{3,1,2,0:T(8,128)(2,1)S(1)}, u32[]{:S(2)}, u32[]{:S(2)}) %collective-permute-start.27) | collective-permute-done | bytes 524320 | tf_op jit(solution)/shard_map/ppermute | solution.py:18
  697.3 3.8 collective-permute-start.19
  701.2 47.7 %collective-permute-start.18 = (bf16[2,256,8,128]{3,1,2,0:T(8,128)(2,1)S(1)}, bf16[2,256,8,128]{3,1,2,0:T(8,128)(2,1)S(1)}, u32[]{:S(2)}, u32[]{:S(2)}) collective-permute-start(bf16[2,256,8,128]{3,1,2,0:T(8,128)(2,1)S(1)} %copy-done.55), channel_id=1, source_target_pairs={{24,0},{32,8},{40,16},{48,24},{56,32},{64,40},{72,48},{80,56},{88,... | collective-permute-start | bytes 3145736 | tf_op jit(solution)/shard_map/ppermute | solution.py:18
  748.9 3.4 collective-permute-start.17
  755.0 2.8 select_bitcast_fusion.1
  759.8 73.0 %collective-permute-done.19 = bf16[2,256,8,128]{3,1,2,0:T(8,128)(2,1)S(1)} collective-permute-done((bf16[2,256,8,128]{3,1,2,0:T(8,128)(2,1)S(1)}, bf16[2,256,8,128]{3,1,2,0:T(8,128)(2,1)S(1)}, u32[]{:S(2)}, u32[]{:S(2)}) %collective-permute-start.19) | collective-permute-done | bytes 1048608 | tf_op jit(solution)/shard_map/ppermute | solution.py:18
  832.8 11.7 %collective-permute-done.18 = bf16[2,256,8,128]{3,1,2,0:T(8,128)(2,1)S(1)} collective-permute-done((bf16[2,256,8,128]{3,1,2,0:T(8,128)(2,1)S(1)}, bf16[2,256,8,128]{3,1,2,0:T(8,128)(2,1)S(1)}, u32[]{:S(2)}, u32[]{:S(2)}) %collective-permute-start.18) | collective-permute-done | bytes 1048608 | tf_op jit(solution)/shard_map/ppermute | solution.py:18
  (741 shorter events, 248.1 us)
Async XLA Ops:
  7.2 204.4 %all-gather.2.cloned.1.call-start = ((), (), s32[]{:S(2)}) async-start(), calls=%async_computation | async-start | bytes 4718592 | tf_op jit(solution)/shard_map/all_gather | solution.py:227
  10.4 464.2 %copy-start.140 = (pred[8]{0:T(512)(128)(4,1)}, pred[8]{0:T(512)(128)(4,1)S(1)}, u32[]{:S(2)}) copy-start(pred[8]{0:T(512)(128)(4,1)S(1)} %get-tuple-element.61) | copy-start | bytes 28
  10.4 429.5 %copy-start.138 = (pred[8]{0:T(512)(128)(4,1)}, pred[8]{0:T(512)(128)(4,1)S(1)}, u32[]{:S(2)}) copy-start(pred[8]{0:T(512)(128)(4,1)S(1)} %get-tuple-element.232) | copy-start | bytes 28
  12.8 149.0 %collective-permute-start.3 = (bf16[2,256,8,128]{3,1,2,0:T(8,128)(2,1)}, bf16[2,256,8,128]{3,1,2,0:T(8,128)(2,1)S(1)}, u32[]{:S(2)}, u32[]{:S(2)}) collective-permute-start(bf16[2,256,8,128]{3,1,2,0:T(8,128)(2,1)} %pad_maximum_fusion.1), channel_id=1, source_target_pairs={{0,32},{8,40},{16,48},{24,56},{32,64},{40,72},{48,80},{56,88},{64,... | collective-permute-start | bytes 3145736 | tf_op jit(solution)/shard_map/ppermute | solution.py:18
  15.1 143.0 %collective-permute-start.2 = (bf16[2,256,8,128]{3,1,2,0:T(8,128)(2,1)}, bf16[2,256,8,128]{3,1,2,0:T(8,128)(2,1)}, u32[]{:S(2)}, u32[]{:S(2)}) collective-permute-start(bf16[2,256,8,128]{3,1,2,0:T(8,128)(2,1)} %pad_maximum_fusion.1), channel_id=1, source_target_pairs={{0,24},{8,32},{16,40},{24,48},{32,56},{40,64},{48,72},{56,80},{64,... | collective-permute-start | bytes 3145736 | tf_op jit(solution)/shard_map/ppermute | solution.py:18
  20.9 133.6 %collective-permute-start.1 = (bf16[2,256,8,128]{3,1,2,0:T(8,128)(2,1)}, bf16[2,256,8,128]{3,1,2,0:T(8,128)(2,1)}, u32[]{:S(2)}, u32[]{:S(2)}) collective-permute-start(bf16[2,256,8,128]{3,1,2,0:T(8,128)(2,1)} %pad_maximum_fusion.1), channel_id=1, source_target_pairs={{0,16},{8,24},{16,32},{24,40},{32,48},{40,56},{48,64},{56,72},{64,... | collective-permute-start | bytes 3145736 | tf_op jit(solution)/shard_map/ppermute | solution.py:18
  22.8 128.0 %collective-permute-start = (bf16[2,256,8,128]{3,1,2,0:T(8,128)(2,1)}, bf16[2,256,8,128]{3,1,2,0:T(8,128)(2,1)}, u32[]{:S(2)}, u32[]{:S(2)}) collective-permute-start(bf16[2,256,8,128]{3,1,2,0:T(8,128)(2,1)} %pad_maximum_fusion.1), channel_id=1, source_target_pairs={{0,8},{8,16},{16,24},{24,32},{32,40},{40,48},{48,56},{56,64},{64,7... | collective-permute-start | bytes 3145736 | tf_op jit(solution)/shard_map/ppermute | solution.py:18
  27.4 432.3 %copy-start.123 = (s32[8,128]{1,0:T(8,128)}, s32[8,128]{1,0:T(8,128)S(1)}, u32[]{:S(2)}) copy-start(s32[8,128]{1,0:T(8,128)S(1)} %get-tuple-element.177) | copy-start | bytes 12292
  27.4 434.5 %copy-start.125 = (s32[8,128]{1,0:T(8,128)}, s32[8,128]{1,0:T(8,128)S(1)}, u32[]{:S(2)}) copy-start(s32[8,128]{1,0:T(8,128)S(1)} %get-tuple-element.176) | copy-start | bytes 12292
  27.4 436.7 %copy-start.127 = (s32[8,128]{1,0:T(8,128)}, s32[8,128]{1,0:T(8,128)S(1)}, u32[]{:S(2)}) copy-start(s32[8,128]{1,0:T(8,128)S(1)} %get-tuple-element.175) | copy-start | bytes 12292
  27.6 430.6 %copy-start.156 = (s32[8,128]{1,0:T(8,128)}, s32[8,128]{1,0:T(8,128)S(1)}, u32[]{:S(2)}) copy-start(s32[8,128]{1,0:T(8,128)S(1)} %get-tuple-element.35) | copy-start | bytes 12292
  27.6 432.1 %copy-start.158 = (s32[8,128]{1,0:T(8,128)}, s32[8,128]{1,0:T(8,128)S(1)}, u32[]{:S(2)}) copy-start(s32[8,128]{1,0:T(8,128)S(1)} %get-tuple-element.34) | copy-start | bytes 12292
  27.6 434.3 %copy-start.160 = (s32[8,128]{1,0:T(8,128)}, s32[8,128]{1,0:T(8,128)S(1)}, u32[]{:S(2)}) copy-start(s32[8,128]{1,0:T(8,128)S(1)} %get-tuple-element.33) | copy-start | bytes 12292
  27.6 438.8 %copy-start.144 = (s32[8,128]{1,0:T(8,128)}, s32[8,128]{1,0:T(8,128)S(1)}, u32[]{:S(2)}) copy-start(s32[8,128]{1,0:T(8,128)S(1)} %get-tuple-element.42) | copy-start | bytes 12292
  27.6 440.8 %copy-start.146 = (s32[8,128]{1,0:T(8,128)}, s32[8,128]{1,0:T(8,128)S(1)}, u32[]{:S(2)}) copy-start(s32[8,128]{1,0:T(8,128)S(1)} %get-tuple-element.41) | copy-start | bytes 12292
  27.6 442.9 %copy-start.148 = (s32[8,128]{1,0:T(8,128)}, s32[8,128]{1,0:T(8,128)S(1)}, u32[]{:S(2)}) copy-start(s32[8,128]{1,0:T(8,128)S(1)} %get-tuple-element.40) | copy-start | bytes 12292
  27.6 444.9 %copy-start.150 = (s32[8,128]{1,0:T(8,128)}, s32[8,128]{1,0:T(8,128)S(1)}, u32[]{:S(2)}) copy-start(s32[8,128]{1,0:T(8,128)S(1)} %get-tuple-element.39) | copy-start | bytes 12292
  36.3 440.9 %copy-start.131 = (s32[8,256]{1,0:T(8,128)}, s32[8,256]{1,0:T(8,128)S(1)}, u32[]{:S(2)}) copy-start(s32[8,256]{1,0:T(8,128)S(1)} %get-tuple-element.46) | copy-start | bytes 24580
  36.3 445.4 %copy-start.129 = (s32[8,256]{1,0:T(8,128)}, s32[8,256]{1,0:T(8,128)S(1)}, u32[]{:S(2)}) copy-start(s32[8,256]{1,0:T(8,128)S(1)} %get-tuple-element.47) | copy-start | bytes 24580
  36.3 448.5 %copy-start.136 = (s32[8,256]{1,0:T(8,128)}, s32[8,256]{1,0:T(8,128)S(1)}, u32[]{:S(2)}) copy-start(s32[8,256]{1,0:T(8,128)S(1)} %get-tuple-element.44) | copy-start | bytes 24580
  165.5 61.5 %collective-permute-start.15 = (bf16[2,128,8,128]{3,1,2,0:T(8,128)(2,1)}, bf16[2,128,8,128]{3,1,2,0:T(8,128)(2,1)}, u32[]{:S(2)}, u32[]{:S(2)}) collective-permute-start(bf16[2,128,8,128]{3,1,2,0:T(8,128)(2,1)} %get-tuple-element.166), channel_id=1, source_target_pairs={{0,128},{8,136},{16,144},{24,152},{32,160},{40,168},{48,176},{56,1... | collective-permute-start | bytes 1572872 | tf_op jit(solution)/shard_map/ppermute | solution.py:18
  167.6 63.6 %collective-permute-start.14 = (bf16[2,128,8,128]{3,1,2,0:T(8,128)(2,1)}, bf16[2,128,8,128]{3,1,2,0:T(8,128)(2,1)}, u32[]{:S(2)}, u32[]{:S(2)}) collective-permute-start(bf16[2,128,8,128]{3,1,2,0:T(8,128)(2,1)} %get-tuple-element.166), channel_id=1, source_target_pairs={{0,120},{8,128},{16,136},{24,144},{32,152},{40,160},{48,168},{56,1... | collective-permute-start | bytes 1572872 | tf_op jit(solution)/shard_map/ppermute | solution.py:18
  170.2 65.1 %collective-permute-start.13 = (bf16[2,128,8,128]{3,1,2,0:T(8,128)(2,1)}, bf16[2,128,8,128]{3,1,2,0:T(8,128)(2,1)}, u32[]{:S(2)}, u32[]{:S(2)}) collective-permute-start(bf16[2,128,8,128]{3,1,2,0:T(8,128)(2,1)} %get-tuple-element.166), channel_id=1, source_target_pairs={{0,112},{8,120},{16,128},{24,136},{32,144},{40,152},{48,160},{56,1... | collective-permute-start | bytes 1572872 | tf_op jit(solution)/shard_map/ppermute | solution.py:18
  192.9 60.9 %collective-permute-start.12 = (bf16[2,128,8,128]{3,1,2,0:T(8,128)(2,1)}, bf16[2,128,8,128]{3,1,2,0:T(8,128)(2,1)}, u32[]{:S(2)}, u32[]{:S(2)}) collective-permute-start(bf16[2,128,8,128]{3,1,2,0:T(8,128)(2,1)} %get-tuple-element.166), channel_id=1, source_target_pairs={{0,104},{8,112},{16,120},{24,128},{32,136},{40,144},{48,152},{56,1... | collective-permute-start | bytes 1572872 | tf_op jit(solution)/shard_map/ppermute | solution.py:18
  209.5 58.5 %collective-permute-start.11 = (bf16[2,128,8,128]{3,1,2,0:T(8,128)(2,1)}, bf16[2,128,8,128]{3,1,2,0:T(8,128)(2,1)}, u32[]{:S(2)}, u32[]{:S(2)}) collective-permute-start(bf16[2,128,8,128]{3,1,2,0:T(8,128)(2,1)} %get-tuple-element.166), channel_id=1, source_target_pairs={{0,96},{8,104},{16,112},{24,120},{32,128},{40,136},{48,144},{56,15... | collective-permute-start | bytes 1572872 | tf_op jit(solution)/shard_map/ppermute | solution.py:18
  226.9 80.1 %collective-permute-start.10 = (bf16[2,128,8,128]{3,1,2,0:T(8,128)(2,1)}, bf16[2,128,8,128]{3,1,2,0:T(8,128)(2,1)S(1)}, u32[]{:S(2)}, u32[]{:S(2)}) collective-permute-start(bf16[2,128,8,128]{3,1,2,0:T(8,128)(2,1)} %get-tuple-element.166), channel_id=1, source_target_pairs={{0,88},{8,96},{16,104},{24,112},{32,120},{40,128},{48,136},{56,144... | collective-permute-start | bytes 1572872 | tf_op jit(solution)/shard_map/ppermute | solution.py:18
  231.1 82.3 %collective-permute-start.9 = (bf16[2,128,8,128]{3,1,2,0:T(8,128)(2,1)}, bf16[2,128,8,128]{3,1,2,0:T(8,128)(2,1)S(1)}, u32[]{:S(2)}, u32[]{:S(2)}) collective-permute-start(bf16[2,128,8,128]{3,1,2,0:T(8,128)(2,1)} %get-tuple-element.166), channel_id=1, source_target_pairs={{0,80},{8,88},{16,96},{24,104},{32,112},{40,120},{48,128},{56,136}... | collective-permute-start | bytes 1572872 | tf_op jit(solution)/shard_map/ppermute | solution.py:18
  235.4 91.5 %collective-permute-start.8 = (bf16[2,128,8,128]{3,1,2,0:T(8,128)(2,1)}, bf16[2,128,8,128]{3,1,2,0:T(8,128)(2,1)S(1)}, u32[]{:S(2)}, u32[]{:S(2)}) collective-permute-start(bf16[2,128,8,128]{3,1,2,0:T(8,128)(2,1)} %get-tuple-element.166), channel_id=1, source_target_pairs={{0,72},{8,80},{16,88},{24,96},{32,104},{40,112},{48,120},{56,128},... | collective-permute-start | bytes 1572872 | tf_op jit(solution)/shard_map/ppermute | solution.py:18
  253.9 74.4 %collective-permute-start.7 = (bf16[2,128,8,128]{3,1,2,0:T(8,128)(2,1)}, bf16[2,128,8,128]{3,1,2,0:T(8,128)(2,1)S(1)}, u32[]{:S(2)}, u32[]{:S(2)}) collective-permute-start(bf16[2,128,8,128]{3,1,2,0:T(8,128)(2,1)} %get-tuple-element.166), channel_id=1, source_target_pairs={{0,64},{8,72},{16,80},{24,88},{32,96},{40,104},{48,112},{56,120},{... | collective-permute-start | bytes 1572872 | tf_op jit(solution)/shard_map/ppermute | solution.py:18
  268.0 89.7 %collective-permute-start.6 = (bf16[2,128,8,128]{3,1,2,0:T(8,128)(2,1)}, bf16[2,128,8,128]{3,1,2,0:T(8,128)(2,1)S(1)}, u32[]{:S(2)}, u32[]{:S(2)}) collective-permute-start(bf16[2,128,8,128]{3,1,2,0:T(8,128)(2,1)} %get-tuple-element.166), channel_id=1, source_target_pairs={{0,56},{8,64},{16,72},{24,80},{32,88},{40,96},{48,104},{56,112},{6... | collective-permute-start | bytes 1572872 | tf_op jit(solution)/shard_map/ppermute | solution.py:18
  307.0 73.6 %collective-permute-start.5 = (bf16[2,128,8,128]{3,1,2,0:T(8,128)(2,1)}, bf16[2,128,8,128]{3,1,2,0:T(8,128)(2,1)S(1)}, u32[]{:S(2)}, u32[]{:S(2)}) collective-permute-start(bf16[2,128,8,128]{3,1,2,0:T(8,128)(2,1)} %get-tuple-element.166), channel_id=1, source_target_pairs={{0,48},{8,56},{16,64},{24,72},{32,80},{40,88},{48,96},{56,104},{64... | collective-permute-start | bytes 1572872 | tf_op jit(solution)/shard_map/ppermute | solution.py:18
  313.4 78.4 %collective-permute-start.4 = (bf16[2,128,8,128]{3,1,2,0:T(8,128)(2,1)}, bf16[2,128,8,128]{3,1,2,0:T(8,128)(2,1)S(1)}, u32[]{:S(2)}, u32[]{:S(2)}) collective-permute-start(bf16[2,128,8,128]{3,1,2,0:T(8,128)(2,1)} %get-tuple-element.166), channel_id=1, source_target_pairs={{0,40},{8,48},{16,56},{24,64},{32,72},{40,80},{48,88},{56,96},{64,... | collective-permute-start | bytes 1572872 | tf_op jit(solution)/shard_map/ppermute | solution.py:18
  553.2 72.6 %collective-permute-start.31 = (bf16[2,128,8,128]{3,1,2,0:T(8,128)(2,1)S(1)}, bf16[2,128,8,128]{3,1,2,0:T(8,128)(2,1)S(1)}, u32[]{:S(2)}, u32[]{:S(2)}) collective-permute-start(bf16[2,128,8,128]{3,1,2,0:T(8,128)(2,1)S(1)} %pad_maximum_fusion.33), channel_id=1, source_target_pairs={{128,0},{136,8},{144,16},{152,24},{160,32},{168,40},{176,48},{184,... | collective-permute-start | bytes 1572872 | tf_op jit(solution)/shard_map/ppermute | solution.py:18
  554.5 74.0 %collective-permute-start.20 = (bf16[2,128,8,128]{3,1,2,0:T(8,128)(2,1)S(1)}, bf16[2,128,8,128]{3,1,2,0:T(8,128)(2,1)S(1)}, u32[]{:S(2)}, u32[]{:S(2)}) collective-permute-start(bf16[2,128,8,128]{3,1,2,0:T(8,128)(2,1)S(1)} %pad_maximum_fusion.22), channel_id=1, source_target_pairs={{40,0},{48,8},{56,16},{64,24},{72,32},{80,40},{88,48},{96,56},{104... | collective-permute-start | bytes 1572872 | tf_op jit(solution)/shard_map/ppermute | solution.py:18
  576.1 56.6 %collective-permute-start.30 = (bf16[2,128,8,128]{3,1,2,0:T(8,128)(2,1)S(1)}, bf16[2,128,8,128]{3,1,2,0:T(8,128)(2,1)S(1)}, u32[]{:S(2)}, u32[]{:S(2)}) collective-permute-start(bf16[2,128,8,128]{3,1,2,0:T(8,128)(2,1)S(1)} %pad_maximum_fusion.32), channel_id=1, source_target_pairs={{120,0},{128,8},{136,16},{144,24},{152,32},{160,40},{168,48},{176,... | collective-permute-start | bytes 1572872 | tf_op jit(solution)/shard_map/ppermute | solution.py:18
  578.1 56.6 %collective-permute-start.29 = (bf16[2,128,8,128]{3,1,2,0:T(8,128)(2,1)S(1)}, bf16[2,128,8,128]{3,1,2,0:T(8,128)(2,1)S(1)}, u32[]{:S(2)}, u32[]{:S(2)}) collective-permute-start(bf16[2,128,8,128]{3,1,2,0:T(8,128)(2,1)S(1)} %pad_maximum_fusion.31), channel_id=1, source_target_pairs={{112,0},{120,8},{128,16},{136,24},{144,32},{152,40},{160,48},{168,... | collective-permute-start | bytes 1572872 | tf_op jit(solution)/shard_map/ppermute | solution.py:18
  581.7 54.9 %collective-permute-start.28 = (bf16[2,128,8,128]{3,1,2,0:T(8,128)(2,1)S(1)}, bf16[2,128,8,128]{3,1,2,0:T(8,128)(2,1)S(1)}, u32[]{:S(2)}, u32[]{:S(2)}) collective-permute-start(bf16[2,128,8,128]{3,1,2,0:T(8,128)(2,1)S(1)} %pad_maximum_fusion.30), channel_id=1, source_target_pairs={{104,0},{112,8},{120,16},{128,24},{136,32},{144,40},{152,48},{160,... | collective-permute-start | bytes 1572872 | tf_op jit(solution)/shard_map/ppermute | solution.py:18
  625.8 57.7 %collective-permute-start.27 = (bf16[2,128,8,128]{3,1,2,0:T(8,128)(2,1)S(1)}, bf16[2,128,8,128]{3,1,2,0:T(8,128)(2,1)S(1)}, u32[]{:S(2)}, u32[]{:S(2)}) collective-permute-start(bf16[2,128,8,128]{3,1,2,0:T(8,128)(2,1)S(1)} %pad_maximum_fusion.29), channel_id=1, source_target_pairs={{96,0},{104,8},{112,16},{120,24},{128,32},{136,40},{144,48},{152,5... | collective-permute-start | bytes 1572872 | tf_op jit(solution)/shard_map/ppermute | solution.py:18
  628.6 64.8 %collective-permute-start.26 = (bf16[2,128,8,128]{3,1,2,0:T(8,128)(2,1)}, bf16[2,128,8,128]{3,1,2,0:T(8,128)(2,1)}, u32[]{:S(2)}, u32[]{:S(2)}) collective-permute-start(bf16[2,128,8,128]{3,1,2,0:T(8,128)(2,1)} %pad_maximum_fusion.28), channel_id=1, source_target_pairs={{88,0},{96,8},{104,16},{112,24},{120,32},{128,40},{136,48},{144,56... | collective-permute-start | bytes 1572872 | tf_op jit(solution)/shard_map/ppermute | solution.py:18
  632.7 64.6 %collective-permute-start.25 = (bf16[2,128,8,128]{3,1,2,0:T(8,128)(2,1)}, bf16[2,128,8,128]{3,1,2,0:T(8,128)(2,1)}, u32[]{:S(2)}, u32[]{:S(2)}) collective-permute-start(bf16[2,128,8,128]{3,1,2,0:T(8,128)(2,1)} %pad_maximum_fusion.27), channel_id=1, source_target_pairs={{80,0},{88,8},{96,16},{104,24},{112,32},{120,40},{128,48},{136,56}... | collective-permute-start | bytes 1572872 | tf_op jit(solution)/shard_map/ppermute | solution.py:18
  634.7 66.5 %collective-permute-start.24 = (bf16[2,128,8,128]{3,1,2,0:T(8,128)(2,1)}, bf16[2,128,8,128]{3,1,2,0:T(8,128)(2,1)}, u32[]{:S(2)}, u32[]{:S(2)}) collective-permute-start(bf16[2,128,8,128]{3,1,2,0:T(8,128)(2,1)} %pad_maximum_fusion.26), channel_id=1, source_target_pairs={{72,0},{80,8},{88,16},{96,24},{104,32},{112,40},{120,48},{128,56},... | collective-permute-start | bytes 1572872 | tf_op jit(solution)/shard_map/ppermute | solution.py:18
  636.6 112.3 %collective-permute-start.23 = (bf16[2,128,8,128]{3,1,2,0:T(8,128)(2,1)}, bf16[2,128,8,128]{3,1,2,0:T(8,128)(2,1)}, u32[]{:S(2)}, u32[]{:S(2)}) collective-permute-start(bf16[2,128,8,128]{3,1,2,0:T(8,128)(2,1)} %pad_maximum_fusion.25), channel_id=1, source_target_pairs={{64,0},{72,8},{80,16},{88,24},{96,32},{104,40},{112,48},{120,56},{... | collective-permute-start | bytes 1572872 | tf_op jit(solution)/shard_map/ppermute | solution.py:18
  683.6 68.8 %collective-permute-start.22 = (bf16[2,128,8,128]{3,1,2,0:T(8,128)(2,1)}, bf16[2,128,8,128]{3,1,2,0:T(8,128)(2,1)}, u32[]{:S(2)}, u32[]{:S(2)}) collective-permute-start(bf16[2,128,8,128]{3,1,2,0:T(8,128)(2,1)} %pad_maximum_fusion.24), channel_id=1, source_target_pairs={{56,0},{64,8},{72,16},{80,24},{88,32},{96,40},{104,48},{112,56},{1... | collective-permute-start | bytes 1572872 | tf_op jit(solution)/shard_map/ppermute | solution.py:18
  693.4 61.6 %collective-permute-start.21 = (bf16[2,128,8,128]{3,1,2,0:T(8,128)(2,1)S(1)}, bf16[2,128,8,128]{3,1,2,0:T(8,128)(2,1)S(1)}, u32[]{:S(2)}, u32[]{:S(2)}) collective-permute-start(bf16[2,128,8,128]{3,1,2,0:T(8,128)(2,1)S(1)} %pad_maximum_fusion.23), channel_id=1, source_target_pairs={{48,0},{56,8},{64,16},{72,24},{80,32},{88,40},{96,48},{104,56},{11... | collective-permute-start | bytes 1572872 | tf_op jit(solution)/shard_map/ppermute | solution.py:18
  697.3 135.5 %collective-permute-start.19 = (bf16[2,256,8,128]{3,1,2,0:T(8,128)(2,1)S(1)}, bf16[2,256,8,128]{3,1,2,0:T(8,128)(2,1)S(1)}, u32[]{:S(2)}, u32[]{:S(2)}) collective-permute-start(bf16[2,256,8,128]{3,1,2,0:T(8,128)(2,1)S(1)} %copy-done.56), channel_id=1, source_target_pairs={{32,0},{40,8},{48,16},{56,24},{64,32},{72,40},{80,48},{88,56},{96,... | collective-permute-start | bytes 3145736 | tf_op jit(solution)/shard_map/ppermute | solution.py:18
  701.2 143.4 %collective-permute-start.18 = (bf16[2,256,8,128]{3,1,2,0:T(8,128)(2,1)S(1)}, bf16[2,256,8,128]{3,1,2,0:T(8,128)(2,1)S(1)}, u32[]{:S(2)}, u32[]{:S(2)}) collective-permute-start(bf16[2,256,8,128]{3,1,2,0:T(8,128)(2,1)S(1)} %copy-done.55), channel_id=1, source_target_pairs={{24,0},{32,8},{40,16},{48,24},{56,32},{64,40},{72,48},{80,56},{88,... | collective-permute-start | bytes 3145736 | tf_op jit(solution)/shard_map/ppermute | solution.py:18
  748.9 95.6 %collective-permute-start.17 = (bf16[2,256,8,128]{3,1,2,0:T(8,128)(2,1)S(1)}, bf16[2,256,8,128]{3,1,2,0:T(8,128)(2,1)S(1)}, u32[]{:S(2)}, u32[]{:S(2)}) collective-permute-start(bf16[2,256,8,128]{3,1,2,0:T(8,128)(2,1)S(1)} %copy-done.54), channel_id=1, source_target_pairs={{16,0},{24,8},{32,16},{40,24},{48,32},{56,40},{64,48},{72,56},{80,... | collective-permute-start | bytes 3145736 | tf_op jit(solution)/shard_map/ppermute | solution.py:18
  752.4 92.1 %collective-permute-start.16 = (bf16[2,256,8,128]{3,1,2,0:T(8,128)(2,1)S(1)}, bf16[2,256,8,128]{3,1,2,0:T(8,128)(2,1)S(1)}, u32[]{:S(2)}, u32[]{:S(2)}) collective-permute-start(bf16[2,256,8,128]{3,1,2,0:T(8,128)(2,1)S(1)} %copy-done.53), channel_id=1, source_target_pairs={{8,0},{16,8},{24,16},{32,24},{40,32},{48,40},{56,48},{64,56},{72,6... | collective-permute-start | bytes 3145736 | tf_op jit(solution)/shard_map/ppermute | solution.py:18
  (212 other events, 7597.7 us)
Sparse Core Ops, SparseCore 0:
  10.7 132.4 all-gather.1
where the time goes:
time: 871 us; the launch traced here: 861 us
  waiting for transfers between devices  359 us (41%)
  starting transfers between devices  187 us (21%)
  matrix products  182 us (21%)
  other arithmetic  57.8 us (7%)
  local copies, waits for them, and re-layouts  56.4 us (6%)
  between operations  19 us (2%)
    ppermute x32, waiting for transfers between devices, passed_along(): return lax.ppermute(value, axis, pairs)  358 us
    ppermute x32, starting transfers between devices, passed_along(): return lax.ppermute(value, axis, pairs)  187 us
    dot_general x132, matrix products, product(): jnp.einsum(pattern, left_operand, right_operand, preferred_element_type=j...  177 us
    reduce_sum x8, other arithmetic, shard_grads(): total_here = total_here + jnp.sum(weights, axis=-1)  28.3 us
    unnamed x468, local copies, waits for them, and re-layouts  20.5 us
  transfers between devices with their start and end apart: 33, of which 12 were waited for; matrix products, arithmetic and copies ran while one was open for 14% of the time, Pallas kernels for 0%

commit v1 on v0

v1 whole, which is shorter than its diff:
```python
import functools
import math

import jax
import jax.numpy as jnp
from jax import lax
from jax.experimental import pallas as pl
from jax.experimental.pallas import tpu as pltpu
from jax.sharding import PartitionSpec as P

HEADS = 8
HS = 128
TOK = 512
ROWS = 256
LROWS = 128
RING = 8
ROW_LINES = 4
NEG = -1e30
SCALE = 1.0 / math.sqrt(HS)
NT = (((1,), (1,)), ((), ()))
NN = (((1,), (0,)), ((), ()))
TN = (((0,), (0,)), ((), ()))
VMEM_LIMIT = 56 * 1024 * 1024


def dot(a, b, dims):
    return lax.dot_general(a, b, dims, preferred_element_type=jnp.float32)


def token_of(row, phase):
    other = jnp.where(phase < 2, phase + 2, phase - 2)
    return 4 * (row & (LROWS - 1)) + jnp.where(row < LROWS, phase, other)


def pick_matrix(phase):
    row = lax.broadcasted_iota(jnp.int32, (ROWS, TOK), 0)
    tok = lax.broadcasted_iota(jnp.int32, (ROWS, TOK), 1)
    return (tok == token_of(row, phase)).astype(jnp.float32).astype(jnp.bfloat16)


def spread_matrix(phase):
    row = lax.broadcasted_iota(jnp.int32, (TOK, ROWS), 1)
    tok = lax.broadcasted_iota(jnp.int32, (TOK, ROWS), 0)
    return (tok == token_of(row, phase)).astype(jnp.float32).astype(jnp.bfloat16)


def place():
    me = lax.axis_index("seq")
    return me, me // RING, lax.rem(me, RING)


def greet(line, pos, with_lines):
    barrier = pltpu.get_barrier_semaphore()
    for o in range(1, RING):
        pl.semaphore_signal(
            barrier, inc=1, device_id={"seq": line * RING + lax.rem(pos + o, RING)}
        )
    if with_lines:
        for o in (1, ROW_LINES - 1):
            pl.semaphore_signal(
                barrier, inc=1, device_id={"seq": lax.rem(line + o, ROW_LINES) * RING + pos}
            )
    pl.semaphore_wait(barrier, RING - 1 + (2 if with_lines else 0))


def send_qkv(
    phase_ref, q_ref, k_ref, v_ref, qo_ref, kvo_ref, stage, send_sem, recv_sem, hsend, hrecv
):
    me, line, pos = place()
    greet(line, pos, True)

    def packed(h):
        pick = pick_matrix(phase_ref[h])
        cols = pl.ds(pl.multiple_of(h * HS, HS), HS)
        return [dot(pick, ref[:, cols], NN).astype(jnp.bfloat16) for ref in (q_ref, k_ref, v_ref)]

    def to_peer(o, what):
        peer = line * RING + lax.rem(pos + o, RING)
        if what == 0:
            src, dst = stage.at[o, 0], qo_ref.at[pos]
        else:
            src, dst = stage.at[o, pl.ds(1, 2)], kvo_ref.at[RING + pos]
        return pltpu.make_async_remote_copy(
            src_ref=src,
            dst_ref=dst,
            send_sem=send_sem.at[what, o],
            recv_sem=recv_sem.at[what, o],
            device_id={"seq": peer},
        )

    def far(s):
        return pltpu.make_async_remote_copy(
            src_ref=kvo_ref.at[RING + s],
            dst_ref=kvo_ref.at[s],
            send_sem=hsend.at[s],
            recv_sem=hrecv.at[s],
            device_id={"seq": me + RING},
        )

    def far_long(s):
        return pltpu.make_async_remote_copy(
            src_ref=kvo_ref.at[RING + s, :, pl.ds(0, LROWS)],
            dst_ref=kvo_ref.at[s, :, pl.ds(0, LROWS)],
            send_sem=hsend.at[s],
            recv_sem=hrecv.at[s],
            device_id={"seq": me + RING},
        )

    def start(o, _):
        for i, rows in enumerate(packed(lax.rem(pos + o, RING))):
            stage[o, i] = rows
        to_peer(o, 1).start()
        to_peer(o, 0).start()
        return 0

    lax.fori_loop(1, RING, start, 0)
    own = packed(pos)
    qo_ref[pos] = own[0]
    kvo_ref[RING + pos, 0] = own[1]
    kvo_ref[RING + pos, 1] = own[2]

    def forward(o, _):
        s = lax.rem(pos + RING - o, RING)

        @pl.when(o > 0)
        def _():
            to_peer(o, 1).wait_recv()

        @pl.when((line < ROW_LINES - 1) & (s >= RING // 2))
        def _():
            far(s).start()

        @pl.when((lax.rem(line, 2) == 0) & (s < RING // 2))
        def _():
            far_long(s).start()

        return 0

    lax.fori_loop(0, RING, forward, 0)

    def finish(o, _):
        to_peer(o, 0).wait_recv()
        to_peer(o, 0).wait_send()
        to_peer(o, 1).wait_send()
        return 0

    lax.fori_loop(1, RING, finish, 0)

    def finish_far(s, _):
        @pl.when((line < ROW_LINES - 1) & (s >= RING // 2))
        def _():
            far(s).wait_send()

        @pl.when((lax.rem(line, 2) == 0) & (s < RING // 2))
        def _():
            far_long(s).wait_send()

        @pl.when((line > 0) & (s >= RING // 2))
        def _():
            far(s).wait_recv()

        @pl.when((lax.rem(line, 2) == 1) & (s < RING // 2))
        def _():
            far_long(s).wait_recv()

        return 0

    lax.fori_loop(0, RING, finish_far, 0)


def send_grad(phase_ref, g_ref, w_ref, out_ref, stage, send_sem, recv_sem):
    me, line, pos = place()
    greet(line, pos, False)

    def packed(h):
        rows = pl.ds(pl.multiple_of(h * HS, HS), HS)
        full = dot(g_ref[...], w_ref[rows, :], NT).astype(jnp.bfloat16)
        return dot(pick_matrix(phase_ref[h]), full, NN).astype(jnp.bfloat16)

    def to_peer(o):
        return pltpu.make_async_remote_copy(
            src_ref=stage.at[o],
            dst_ref=out_ref.at[pos],
            send_sem=send_sem.at[o],
            recv_sem=recv_sem.at[o],
            device_id={"seq": line * RING + lax.rem(pos + o, RING)},
        )

    def start(o, _):
        stage[o] = packed(lax.rem(pos + o, RING))
        to_peer(o).start()
        return 0

    lax.fori_loop(1, RING, start, 0)
    out_ref[pos] = packed(pos)

    def finish(o, _):
        to_peer(o).wait_recv()
        to_peer(o).wait_send()
        return 0

    lax.fori_loop(1, RING, finish, 0)


def attend(sc_ref, q_ref, kv_ref, do_ref, dq_ref, own_ref, far_ref, acc, s_sc, dp_sc, sl_sc, dpl_sc):
    phase = sc_ref[0]
    seq_start = sc_ref[1]
    acc[...] = jnp.zeros_like(acc)

    def low_of(tok, first, count):
        low = jnp.full_like(tok, seq_start)
        for n in range(count):
            end = sc_ref[first + n]
            low = jnp.where(tok >= end, jnp.maximum(low, end), low)
        return low

    def scalar_low(tok, first, count):
        low = seq_start
        for n in range(count):
            end = sc_ref[first + n]
            low = jnp.where(tok >= end, jnp.maximum(low, end), low)
        return low

    n_short, n_long = 15, 3
    key_off = token_of(lax.broadcasted_iota(jnp.int32, (ROWS, 1), 0), phase)
    lrow = lax.broadcasted_iota(jnp.int32, (4 * LROWS, 1), 0)
    long_off = (lrow // LROWS) * TOK + 4 * (lrow & (LROWS - 1)) + phase
    query_off = token_of(lax.broadcasted_iota(jnp.int32, (1, ROWS), 1), phase)

    def block(i, _):
        g = RING + i
        q = q_ref[i]
        do = do_ref[i]
        ql, dol = q[:LROWS], do[:LROWS]
        tok = g * TOK + query_off
        tokl = tok[:, :LROWS]
        low_s = low_of(tok, 2, n_short)
        low_l = low_of(tokl, 2 + n_short, n_long)
        first_s = scalar_low(g * TOK, 2, n_short) // TOK
        first_l = scalar_low(g * TOK, 2 + n_short, n_long) // (4 * TOK)
        first_s = jnp.maximum(first_s, g - 4)
        last_l = g // 4 + 1

        def long_kv(c, which):
            return kv_ref[pl.ds(4 * c, 4), which, pl.ds(0, LROWS), :].reshape(4 * LROWS, HS)

        def score(j, m):
            s = dot(kv_ref[j, 0], q, NT)
            u = j * TOK + key_off
            s = jnp.where((u >= low_s) & (u <= tok), s, NEG)
            s_sc[j - g + 4] = s
            return jnp.maximum(m, jnp.max(s, axis=0, keepdims=True))

        m = lax.fori_loop(first_s, g + 1, score, jnp.full((1, ROWS), NEG, jnp.float32))

        def score_long(c, m):
            s = dot(long_kv(c, 0), ql, NT)
            u = c * (4 * TOK) + long_off
            s = jnp.where((u >= low_l) & (u <= tokl), s, NEG)
            sl_sc[c] = s
            return jnp.maximum(m, jnp.max(s, axis=0, keepdims=True))

        ml = lax.fori_loop(first_l, last_l, score_long, m[:, :LROWS])
        m = jnp.concatenate([ml, m[:, LROWS:]], axis=1)

        def weigh(j, carry):
            l, d = carry
            p = jnp.exp((s_sc[j - g + 4] - m) * SCALE)
            dp = dot(kv_ref[j, 1], do, NT)
            s_sc[j - g + 4] = p
            dp_sc[j - g + 4] = dp
            return (
                l + jnp.sum(p, axis=0, keepdims=True),
                d + jnp.sum(p * dp, axis=0, keepdims=True),
            )

        zero = jnp.zeros((1, ROWS), jnp.float32)
        l, d = lax.fori_loop(first_s, g + 1, weigh, (zero, zero))

        def weigh_long(c, carry):
            l, d = carry
            p = jnp.exp((sl_sc[c] - ml) * SCALE)
            dp = dot(long_kv(c, 1), dol, NT)
            sl_sc[c] = p
            dpl_sc[c] = dp
            return (
                l + jnp.sum(p, axis=0, keepdims=True),
                d + jnp.sum(p * dp, axis=0, keepdims=True),
            )

        ll, dl = lax.fori_loop(first_l, last_l, weigh_long, (l[:, :LROWS], d[:, :LROWS]))
        l = jnp.concatenate([ll, l[:, LROWS:]], axis=1)
        d = jnp.concatenate([dl, d[:, LROWS:]], axis=1)
        inv = 1.0 / l
        delta = d * inv
        invl, deltal = inv[:, :LROWS], delta[:, :LROWS]

        def back(j, dqt):
            pr = s_sc[j - g + 4] * inv
            ds = (pr * (dp_sc[j - g + 4] - delta)).astype(jnp.bfloat16)
            acc[j, 1] += dot(pr.astype(jnp.bfloat16), do, NN)
            acc[j, 0] += dot(ds, q, NN)
            return dqt + dot(kv_ref[j, 0], ds, TN)

        dqt = lax.fori_loop(first_s, g + 1, back, jnp.zeros((HS, ROWS), jnp.float32))

        def back_long(c, dqt):
            pr = sl_sc[c] * invl
            ds = (pr * (dpl_sc[c] - deltal)).astype(jnp.bfloat16)
            dv = dot(pr.astype(jnp.bfloat16), dol, NN)
            dk = dot(ds, ql, NN)
            acc[pl.ds(4 * c, 4), 1, pl.ds(0, LROWS), :] += dv.reshape(4, LROWS, HS)
            acc[pl.ds(4 * c, 4), 0, pl.ds(0, LROWS), :] += dk.reshape(4, LROWS, HS)
            return dqt + dot(long_kv(c, 0), ds, TN)

        dqlt = lax.fori_loop(first_l, last_l, back_long, dqt[:, :LROWS])
        dq_ref[i, pl.ds(0, LROWS), :] = (dqlt.T * SCALE).astype(jnp.bfloat16)
        dq_ref[i, pl.ds(LROWS, LROWS), :] = (dqt[:, LROWS:].T * SCALE).astype(jnp.bfloat16)
        return 0

    lax.fori_loop(0, RING, block, 0)

    def emit(b, _):
        far_ref[b, 0] = (acc[b, 0] * SCALE).astype(jnp.bfloat16)
        far_ref[b, 1] = acc[b, 1].astype(jnp.bfloat16)
        own_ref[b, 0] = acc[RING + b, 0] * SCALE
        own_ref[b, 1] = acc[RING + b, 1]
        return 0

    lax.fori_loop(0, RING, emit, 0)


def give_back(
    phase_ref,
    dq_ref,
    own_ref,
    far_ref,
    gq_ref,
    gk_ref,
    gv_ref,
    stage,
    near,
    got_q,
    got_kv,
    send_sem,
    recv_sem,
    hsend,
    hrecv,
):
    me, line, pos = place()
    greet(line, pos, True)

    def far(s):
        return pltpu.make_async_remote_copy(
            src_ref=far_ref.at[s],
            dst_ref=near.at[s],
            send_sem=hsend.at[s],
            recv_sem=hrecv.at[s],
            device_id={"seq": me - RING},
        )

    def far_long(s):
        return pltpu.make_async_remote_copy(
            src_ref=far_ref.at[s, :, pl.ds(0, LROWS)],
            dst_ref=near.at[s, :, pl.ds(0, LROWS)],
            send_sem=hsend.at[s],
            recv_sem=hrecv.at[s],
            device_id={"seq": me - RING},
        )

    def home(o, what):
        s = lax.rem(pos + o, RING)
        if what == 0:
            src, dst = dq_ref.at[s], got_q.at[pos]
        else:
            src, dst = stage.at[s], got_kv.at[pos]
        return pltpu.make_async_remote_copy(
            src_ref=src,
            dst_ref=dst,
            send_sem=send_sem.at[what, o],
            recv_sem=recv_sem.at[what, o],
            device_id={"seq": line * RING + s},
        )

    def start_far(o, _):
        s = lax.rem(pos + o, RING)

        @pl.when((line > 0) & (s >= RING // 2))
        def _():
            far(s).start()

        @pl.when((lax.rem(line, 2) == 1) & (s < RING // 2))
        def _():
            far_long(s).start()

        return 0

    lax.fori_loop(1, RING + 1, start_far, 0)

    def start_q(o, _):
        home(o, 0).start()
        return 0

    lax.fori_loop(1, RING, start_q, 0)
    got_q[pos] = dq_ref[pos]

    def start_kv(o, _):
        s = lax.rem(pos + o, RING)
        full = (line < ROW_LINES - 1) & (s >= RING // 2)
        half = (lax.rem(line, 2) == 0) & (s < RING // 2)

        @pl.when(full)
        def _():
            far(s).wait_recv()
            stage[s] = (own_ref[s] + near[s].astype(jnp.float32)).astype(jnp.bfloat16)

        @pl.when(half)
        def _():
            far_long(s).wait_recv()
            stage[s, :, pl.ds(0, LROWS)] = (
                own_ref[s, :, pl.ds(0, LROWS)] + near[s, :, pl.ds(0, LROWS)].astype(jnp.float32)
            ).astype(jnp.bfloat16)
            stage[s, :, pl.ds(LROWS, LROWS)] = own_ref[s, :, pl.ds(LROWS, LROWS)].astype(
                jnp.bfloat16
            )

        @pl.when(jnp.logical_not(full | half))
        def _():
            stage[s] = own_ref[s].astype(jnp.bfloat16)

        @pl.when(o < RING)
        def _():
            home(o, 1).start()

        return 0

    lax.fori_loop(1, RING + 1, start_kv, 0)
    got_kv[pos] = stage[pos]

    def unpack(o, _):
        h = lax.rem(pos + RING - o, RING)

        @pl.when(o > 0)
        def _():
            home(o, 0).wait_recv()
            home(o, 1).wait_recv()

        spread = spread_matrix(phase_ref[h])
        cols = pl.ds(pl.multiple_of(h * HS, HS), HS)
        gq_ref[:, cols] = dot(spread, got_q[h], NN).astype(jnp.bfloat16)
        gk_ref[:, cols] = dot(spread, got_kv[h, 0], NN).astype(jnp.bfloat16)
        gv_ref[:, cols] = dot(spread, got_kv[h, 1], NN).astype(jnp.bfloat16)
        return 0

    lax.fori_loop(0, RING, unpack, 0)

    def finish(o, _):
        home(o, 0).wait_send()
        home(o, 1).wait_send()
        return 0

    lax.fori_loop(1, RING, finish, 0)

    def finish_far(s, _):
        @pl.when((line > 0) & (s >= RING // 2))
        def _():
            far(s).wait_send()

        @pl.when((lax.rem(line, 2) == 1) & (s < RING // 2))
        def _():
            far_long(s).wait_send()

        return 0

    lax.fori_loop(0, RING, finish_far, 0)


VM = pl.BlockSpec(memory_space=pltpu.VMEM)
SM = pl.BlockSpec(memory_space=pltpu.SMEM)
DMA = pltpu.SemaphoreType.DMA
BF = jnp.bfloat16


def shaped(*dims, dtype=BF):
    return jax.ShapeDtypeStruct(dims, dtype)


def shards(q, k, v, grad_mixed, out_weight, head_phase, segments_short, segments_long):
    me = lax.axis_index("seq")
    line, pos = me // RING, lax.rem(me, RING)
    weight = lax.all_gather(out_weight, "fsdp", axis=0, tiled=True)

    q_rows, kv_rows = pl.pallas_call(
        send_qkv,
        out_shape=(shaped(RING, ROWS, HS), shaped(2 * RING, 2, ROWS, HS)),
        in_specs=[SM, VM, VM, VM],
        out_specs=(VM, VM),
        scratch_shapes=[
            pltpu.VMEM((RING, 3, ROWS, HS), BF),
            DMA((2, RING)),
            DMA((2, RING)),
            DMA((RING,)),
            DMA((RING,)),
        ],
        compiler_params=pltpu.CompilerParams(
            collective_id=0, has_side_effects=True, vmem_limit_bytes=VMEM_LIMIT
        ),
        name="send_qkv",
    )(head_phase, q[0], k[0], v[0])

    do_rows = pl.pallas_call(
        send_grad,
        out_shape=shaped(RING, ROWS, HS),
        in_specs=[SM, VM, VM],
        out_specs=VM,
        scratch_shapes=[pltpu.VMEM((RING, ROWS, HS), BF), DMA((RING,)), DMA((RING,))],
        compiler_params=pltpu.CompilerParams(
            collective_id=1, has_side_effects=True, vmem_limit_bytes=VMEM_LIMIT
        ),
        name="send_grad",
    )(head_phase, grad_mixed[0], weight)

    origin = (line - 1) * (RING * TOK)

    def ends(lengths):
        n = lengths.shape[0]
        tri = jnp.arange(n)[None, :] <= jnp.arange(n)[:, None]
        return jnp.sum(jnp.where(tri, lengths[None, :], 0), axis=1) - origin

    phase_here = jnp.sum(jnp.where(jnp.arange(HEADS) == pos, head_phase, 0))
    scalars = jnp.concatenate(
        [jnp.stack([phase_here, -origin]), ends(segments_short), ends(segments_long)]
    ).astype(jnp.int32)
    dq_rows, own, far = pl.pallas_call(
        attend,
        out_shape=(
            shaped(RING, ROWS, HS),
            shaped(RING, 2, ROWS, HS, dtype=jnp.float32),
            shaped(RING, 2, ROWS, HS),
        ),
        in_specs=[SM, VM, VM, VM],
        out_specs=(VM, VM, VM),
        scratch_shapes=[
            pltpu.VMEM((2 * RING, 2, ROWS, HS), jnp.float32),
            pltpu.VMEM((5, ROWS, ROWS), jnp.float32),
            pltpu.VMEM((5, ROWS, ROWS), jnp.float32),
            pltpu.VMEM((4, 4 * LROWS, LROWS), jnp.float32),
            pltpu.VMEM((4, 4 * LROWS, LROWS), jnp.float32),
        ],
        compiler_params=pltpu.CompilerParams(vmem_limit_bytes=VMEM_LIMIT),
        name="attend",
    )(scalars, q_rows, kv_rows, do_rows)

    gq, gk, gv = pl.pallas_call(
        give_back,
        out_shape=(shaped(TOK, HEADS * HS),) * 3,
        in_specs=[SM, VM, VM, VM],
        out_specs=(VM,) * 3,
        scratch_shapes=[
            pltpu.VMEM((RING, 2, ROWS, HS), BF),
            pltpu.VMEM((RING, 2, ROWS, HS), BF),
            pltpu.VMEM((RING, ROWS, HS), BF),
            pltpu.VMEM((RING, 2, ROWS, HS), BF),
            DMA((2, RING)),
            DMA((2, RING)),
            DMA((RING,)),
            DMA((RING,)),
        ],
        compiler_params=pltpu.CompilerParams(
            collective_id=2, has_side_effects=True, vmem_limit_bytes=VMEM_LIMIT
        ),
        name="give_back",
    )(head_phase, dq_rows, own, far)
    return gq[None], gk[None], gv[None]


def solution(mesh):
    placed = (
        P("fsdp", "seq", None),
        P("fsdp", "seq", None),
        P("fsdp", "seq", None),
        P("fsdp", "seq", None),
        P("fsdp", None),
        P(),
        P(),
        P(),
    )
    return jax.shard_map(
        shards,
        mesh=mesh,
        in_specs=placed,
        out_specs=(P("fsdp", "seq", None), P("fsdp", "seq", None), P("fsdp", "seq", None)),
        check_vma=False,
    )
```

time: 871 us -> 248 us (0.28)
  waiting for transfers between devices: 359 us -> 59.2 us
  starting transfers between devices: 187 us -> 0.04 us
  matrix products: 182 us -> 0 us
  Pallas kernels: 0 us -> 165 us
  other arithmetic: 57.8 us -> 2.11 us
  local copies, waits for them, and re-layouts: 56.4 us -> 4.37 us
    ppermute x32 -> x0, waiting for transfers between devices: 358 us -> none  [passed_along(): return lax.ppermute(value, axis, pairs)]
    ppermute x32 -> x0, starting transfers between devices: 187 us -> none  [passed_along(): return lax.ppermute(value, axis, pairs)]
    dot_general x133 -> x0, matrix products: 182 us -> none  [the longest x132 177 us: product(): jnp.einsum(pattern, left_operand, right_operand, preferred_element_type=j...]
    pallas_call x0 -> x4, Pallas kernels: none -> 165 us  [the longest x1 56.8 us: shards(): pl.pallas_call(send_qkv, out_shape=(shaped(RING, ROWS, HS), shaped(2 * RI...]
    all_gather x1, waiting for transfers between devices: 0.02 us -> 58.5 us  [shards(): weight = lax.all_gather(out_weight, 'fsdp', axis=0, tiled=True)]
    reduce_sum x10 -> x3, other arithmetic: 28.5 us -> 0.87 us  [the longest x1 0.64 us: shards(): phase_here = jnp.sum(jnp.where(jnp.arange(HEADS) == pos, head_phase, 0))]
    another operation x21 -> x0, local copies, waits for them, and re-layouts: 21.5 us -> none  [the longest x16 15.3 us: put_half(): stacked = jnp.stack([first_half, second_half], axis=-3)]
    another operation x39 -> x0, other arithmetic: 18 us -> none  [the longest x18 7.68 us: put_half(): stacked = jnp.stack([first_half, second_half], axis=-3)]
  transfers between devices with their start and end apart: 33 -> 1, of which waited for: 12 -> 1; matrix products, arithmetic and copies ran while one was open for 14% -> 1% of each run, Pallas kernels for 0% -> 23%
where the time goes in v1:
time: 248 us; the launch traced here: 245 us
  Pallas kernels  165 us (67%)
  waiting for transfers between devices  59.2 us (24%)
  between operations  14.1 us (6%)
  local copies, waits for them, and re-layouts  4.37 us (2%)
    all_gather x1, waiting for transfers between devices, shards(): weight = lax.all_gather(out_weight, 'fsdp', axis=0, tiled=True)  58.5 us
    pallas_call x1, Pallas kernels, shards(): pl.pallas_call(send_qkv, out_shape=(shaped(RING, ROWS, HS), shaped(2 * RI...  56.8 us
    pallas_call x1, Pallas kernels, shards(): pl.pallas_call(give_back, out_shape=(shaped(TOK, HEADS * HS),) * 3, in_sp...  42.6 us
    pallas_call x1, Pallas kernels, shards(): pl.pallas_call(attend, out_shape=(shaped(RING, ROWS, HS), shaped(RING, 2,...  41.9 us
    pallas_call x1, Pallas kernels, shards(): pl.pallas_call(send_grad, out_shape=shaped(RING, ROWS, HS), in_specs=[SM,...  23.7 us
  transfers between devices with their start and end apart: 1, of which 1 were waited for; matrix products, arithmetic and copies ran while one was open for 1% of the time, Pallas kernels for 23%

profile of v1, /device:TPU:107, one launch (start us, length us, event | category | flops | bytes accessed | tf_op | source)
XLA Modules:
  0.0 245.0 jit_solution(2183309291705782671)
XLA Ops:
  7.2 0.0 copy-start.2
  7.2 0.0 copy-start.3
  7.2 0.0 copy-start.4
  7.2 0.0 all-gather.2.cloned.1.call-start
  7.2 0.7 all-gather.2.cloned.1.call-update
  7.9 56.8 %send_qkv.1 = (bf16[8,256,128]{2,1,0:T(8,128)(2,1)}, bf16[16,2,256,128]{3,2,1,0:T(8,128)(2,1)}) custom-call(s32[8]{0:T(128)} %phase_ref.5, bf16[512,1024]{1,0:T(8,128)(2,1)} %bitcast.10, bf16[512,1024]{1,0:T(8,128)(2,1)} %bitcast.11, bf16[512,1024]{1,0:T(8,128)(2,1)} %bitcast.12), custom_call_target="tpu_custom_call" | custom-call | tf_op jit(solution)/shard_map/send_qkv/pallas_call | solution.py:493
  64.8 0.0 copy-done.2
  64.8 0.6 fusion
  65.4 0.0 copy-done.3
  65.4 0.1 select_reduce_fusion.1
  65.6 0.0 copy-done.4
  65.6 0.1 select_reduce_fusion
  65.7 1.2 pad_add_fusion.sc_ref
  66.9 58.5 %all-gather.2.cloned.1.call-done.w_ref = bf16[1024,2048]{1,0:T(8,128)(2,1)} async-done(((bf16[128,2048]{1,0:T(8,128)(2,1)}), bf16[1024,2048]{1,0:T(8,128)(2,1)}) %all-gather.2.cloned.1.call-update) | async-done | bytes 4194320 | tf_op jit(solution)/shard_map/all_gather | solution.py:491
  125.5 23.7 %send_grad.1.do_ref = bf16[8,256,128]{2,1,0:T(8,128)(2,1)} custom-call(s32[8]{0:T(128)} %phase_ref.5, bf16[512,2048]{1,0:T(8,128)(2,1)} %bitcast.9, bf16[1024,2048]{1,0:T(8,128)(2,1)} %all-gather.2.cloned.1.call-done.w_ref), custom_call_target="tpu_custom_call" | custom-call | tf_op jit(solution)/shard_map/send_grad/pallas_call | solution.py:511
  149.2 41.9 %attend.1 = (bf16[8,256,128]{2,1,0:T(8,128)(2,1)}, f32[8,2,256,128]{3,2,1,0:T(8,128)}, bf16[8,2,256,128]{3,2,1,0:T(8,128)(2,1)}) custom-call(s32[20]{0:T(128)} %pad_add_fusion.sc_ref, bf16[8,256,128]{2,1,0:T(8,128)(2,1)} %get-tuple-element.11.q_ref, bf16[16,2,256,128]{3,2,1,0:T(8,128)(2,1)} %get-tuple-element.12.kv_ref, bf16[8,256,128]{2,1,0:T(8,128)(2,1)} %send_grad.1.do_ref), custom_call_target="tpu_custom_call" | custom-call | tf_op jit(solution)/shard_map/attend/pallas_call | solution.py:534
  191.2 42.6 %give_back.1 = (bf16[512,1024]{1,0:T(8,128)(2,1)}, bf16[512,1024]{1,0:T(8,128)(2,1)}, bf16[512,1024]{1,0:T(8,128)(2,1)}) custom-call(s32[8]{0:T(128)} %phase_ref.5, bf16[8,256,128]{2,1,0:T(8,128)(2,1)} %get-tuple-element.13.dq_ref, f32[8,2,256,128]{3,2,1,0:T(8,128)} %get-tuple-element.14.own_ref, bf16[8,2,256,128]{3,2,1,0:T(8,128)(2,1)} %get-tuple-element.15.far_ref), custom_call_target="tpu_custom_call" | custom-call | tf_op jit(solution)/shard_map/give_back/pallas_call | solution.py:554
  233.7 0.0 copy-start.1
  233.7 0.0 copy-start
  233.7 2.4 copy.14
  236.2 0.0 copy-done.1
  236.2 1.0 copy.15
  237.1 0.0 copy-done
  237.1 1.0 copy.16
  (2 shorter events, 0.0 us)
Async XLA Ops:
  7.2 57.6 %copy-start.2 = (s32[8]{0:T(128)S(1)}, s32[8]{0:T(128)}, u32[]{:S(2)}) copy-start(s32[8]{0:T(128)} %phase_ref.5) | copy-start | bytes 100
  7.2 58.3 %copy-start.3 = (s32[3]{0:T(128)S(1)}, s32[3]{0:T(128)}, u32[]{:S(2)}) copy-start(s32[3]{0:T(128)} %param.15) | copy-start | bytes 40
  7.2 58.4 %copy-start.4 = (s32[15]{0:T(128)S(1)}, s32[15]{0:T(128)}, u32[]{:S(2)}) copy-start(s32[15]{0:T(128)} %param.14) | copy-start | bytes 184
  7.2 118.3 %all-gather.2.cloned.1.call-start = ((), (), s32[]{:S(2)}) async-start(), calls=%async_computation | async-start | bytes 4718592 | tf_op jit(solution)/shard_map/all_gather | solution.py:491
  233.7 2.4 copy-start.1
  233.7 3.4 %copy-start = (bf16[512,1024]{1,0:T(8,128)(2,1)S(1)}, bf16[512,1024]{1,0:T(8,128)(2,1)}, u32[]{:S(2)}) copy-start(bf16[512,1024]{1,0:T(8,128)(2,1)} %get-tuple-element.18) | copy-start | bytes 3145732
Sparse Core Ops, SparseCore 0:
  10.7 114.7 all-gather.1

commit v2 on v1

--- a/solution.py
+++ b/solution.py
@@ -15,6 +15,7 @@
 LROWS = 128
 RING = 8
 ROW_LINES = 4
+XS = 4
 NEG = -1e30
 SCALE = 1.0 / math.sqrt(HS)
 NT = (((1,), (1,)), ((), ()))
@@ -49,25 +50,109 @@
     return me, me // RING, lax.rem(me, RING)
 
 
-def greet(line, pos, with_lines):
+def greet(line, pos, columns, gather):
     barrier = pltpu.get_barrier_semaphore()
     for o in range(1, RING):
         pl.semaphore_signal(
             barrier, inc=1, device_id={"seq": line * RING + lax.rem(pos + o, RING)}
         )
-    if with_lines:
-        for o in (1, ROW_LINES - 1):
-            pl.semaphore_signal(
-                barrier, inc=1, device_id={"seq": lax.rem(line + o, ROW_LINES) * RING + pos}
-            )
-    pl.semaphore_wait(barrier, RING - 1 + (2 if with_lines else 0))
-
-
-def send_qkv(
-    phase_ref, q_ref, k_ref, v_ref, qo_ref, kvo_ref, stage, send_sem, recv_sem, hsend, hrecv
+    for o in columns:
+        pl.semaphore_signal(
+            barrier, inc=1, device_id={"seq": lax.rem(line + o, ROW_LINES) * RING + pos}
+        )
+    total = RING - 1 + len(columns)
+    if gather:
+        f = lax.axis_index("fsdp")
+        x, hi = f // 2, lax.rem(f, 2)
+        pl.semaphore_signal(barrier, inc=1, device_id={"fsdp": 2 * x + 1 - hi})
+        for o in range(1, XS):
+            pl.semaphore_signal(barrier, inc=1, device_id={"fsdp": 2 * lax.rem(x + o, XS) + hi})
+        total += XS
+    pl.semaphore_wait(barrier, total)
+
+
+def send_all(
+    phase_ref,
+    q_ref,
+    k_ref,
+    v_ref,
+    g_ref,
+    w_ref,
+    qo_ref,
+    kvo_ref,
+    do_ref,
+    stage,
+    gstage,
+    w_all,
+    send_sem,
+    recv_sem,
+    hsend,
+    hrecv,
+    gsend,
+    grecv,
+    zsend,
+    zrecv,
+    ysend,
+    yrecv,
+    xsend,
+    xrecv,
+    csend,
+    crecv,
 ):
     me, line, pos = place()
-    greet(line, pos, True)
+    core = lax.rem(me, 2)
+    f = lax.axis_index("fsdp")
+    x, hi = f // 2, lax.rem(f, 2)
+    mate = 2 * x + 1 - hi
+    greet(line, pos, (1, 2, 3), True)
+    half = pl.ds(pl.multiple_of(core * 64, 64), 64)
+    piece = pl.ds(pl.multiple_of(core * 64 + line * 16, 16), 16)
+
+    to_mate = pltpu.make_async_remote_copy(
+        src_ref=w_ref.at[piece],
+        dst_ref=w_all.at[f, piece],
+        send_sem=zsend,
+        recv_sem=zrecv,
+        device_id={"fsdp": mate},
+    )
+
+    def along_y(o):
+        return pltpu.make_async_remote_copy(
+            src_ref=w_all.at[mate, piece],
+            dst_ref=w_all.at[mate, piece],
+            send_sem=ysend.at[o],
+            recv_sem=yrecv.at[o],
+            device_id={"seq": lax.rem(line + o, ROW_LINES) * RING + pos},
+        )
+
+    def along_x(j, own):
+        m = jnp.maximum(j - 2, 0)
+        src = w_ref.at[half] if own else w_all.at[mate, half]
+        return pltpu.make_async_remote_copy(
+            src_ref=src,
+            dst_ref=w_all.at[f if own else mate, half],
+            send_sem=xsend.at[j],
+            recv_sem=xrecv.at[j],
+            device_id={"fsdp": 2 * lax.rem(x + lax.rem(m, 3) + 1, XS) + hi},
+        )
+
+    def slot(j):
+        m = jnp.maximum(j - 2, 0)
+        other = 2 * lax.rem(x + XS - 1 - lax.rem(m, 3), XS) + jnp.where(m < 3, hi, 1 - hi)
+        return jnp.where(j == 0, f, jnp.where(j == 1, mate, other))
+
+    def to_core(j):
+        return pltpu.make_async_remote_copy(
+            src_ref=w_all.at[slot(j), half],
+            dst_ref=w_all.at[slot(j), half],
+            send_sem=csend.at[j],
+            recv_sem=crecv.at[j],
+            device_id={"seq": me + 1 - 2 * core},
+        )
+
+    to_mate.start()
+    for j in range(2, 5):
+        along_x(j, True).start()
 
     def packed(h):
         pick = pick_matrix(phase_ref[h])
@@ -114,10 +199,57 @@
         return 0
 
     lax.fori_loop(1, RING, start, 0)
+
+    to_mate.wait_recv()
+    for o in range(1, ROW_LINES):
+        along_y(o).start()
     own = packed(pos)
     qo_ref[pos] = own[0]
     kvo_ref[RING + pos, 0] = own[1]
     kvo_ref[RING + pos, 1] = own[2]
+    w_all[f] = w_ref[...]
+    for o in range(1, ROW_LINES):
+        along_y(o).wait_recv()
+    for j in range(5, 8):
+        along_x(j, False).start()
+    to_core(1).start()
+
+    def to_head(j, h):
+        return pltpu.make_async_remote_copy(
+            src_ref=gstage.at[j],
+            dst_ref=do_ref.at[pos],
+            send_sem=gsend.at[j],
+            recv_sem=grecv.at[pos],
+            device_id={"seq": line * RING + h},
+        )
+
+    def grad_head(j, _):
+        h = slot(j)
+
+        @pl.when((j >= 1) & (j < RING - 1))
+        def _():
+            along_x(j + 1, True).wait_recv()
+            to_core(j + 1).start()
+
+        @pl.when(j >= 1)
+        def _():
+            to_core(j).wait_recv()
+
+        full = dot(g_ref[...], w_all[h], NT).astype(jnp.bfloat16)
+        rows = dot(pick_matrix(phase_ref[h]), full, NN).astype(jnp.bfloat16)
+
+        @pl.when(h == pos)
+        def _():
+            do_ref[pos] = rows
+
+        @pl.when(h != pos)
+        def _():
+            gstage[j] = rows
+            to_head(j, h).start()
+
+        return 0
+
+    lax.fori_loop(0, RING, grad_head, 0)
 
     def forward(o, _):
         s = lax.rem(pos + RING - o, RING)
@@ -146,6 +278,27 @@
 
     lax.fori_loop(1, RING, finish, 0)
 
+    def finish_grad(j, _):
+        h = slot(j)
+
+        @pl.when(h != pos)
+        def _():
+            to_head(j, h).wait_send()
+
+        @pl.when(j != pos)
+        def _():
+            pltpu.make_async_remote_copy(
+                src_ref=gstage.at[j],
+                dst_ref=do_ref.at[j],
+                send_sem=gsend.at[j],
+                recv_sem=grecv.at[j],
+                device_id={"seq": line * RING + lax.rem(pos + 1, RING)},
+            ).wait_recv()
+
+        return 0
+
+    lax.fori_loop(0, RING, finish_grad, 0)
+
     def finish_far(s, _):
         @pl.when((line < ROW_LINES - 1) & (s >= RING // 2))
         def _():
@@ -166,40 +319,13 @@
         return 0
 
     lax.fori_loop(0, RING, finish_far, 0)
-
-
-def send_grad(phase_ref, g_ref, w_ref, out_ref, stage, send_sem, recv_sem):
-    me, line, pos = place()
-    greet(line, pos, False)
-
-    def packed(h):
-        rows = pl.ds(pl.multiple_of(h * HS, HS), HS)
-        full = dot(g_ref[...], w_ref[rows, :], NT).astype(jnp.bfloat16)
-        return dot(pick_matrix(phase_ref[h]), full, NN).astype(jnp.bfloat16)
-
-    def to_peer(o):
-        return pltpu.make_async_remote_copy(
-            src_ref=stage.at[o],
-            dst_ref=out_ref.at[pos],
-            send_sem=send_sem.at[o],
-            recv_sem=recv_sem.at[o],
-            device_id={"seq": line * RING + lax.rem(pos + o, RING)},
-        )
-
-    def start(o, _):
-        stage[o] = packed(lax.rem(pos + o, RING))
-        to_peer(o).start()
-        return 0
-
-    lax.fori_loop(1, RING, start, 0)
-    out_ref[pos] = packed(pos)
-
-    def finish(o, _):
-        to_peer(o).wait_recv()
-        to_peer(o).wait_send()
-        return 0
-
-    lax.fori_loop(1, RING, finish, 0)
+    to_mate.wait_send()
+    for o in range(1, ROW_LINES):
+        along_y(o).wait_send()
+    for j in range(2, 8):
+        along_x(j, True).wait_send()
+    for j in range(1, 8):
+        to_core(j).wait_send()
 
 
 def attend(sc_ref, q_ref, kv_ref, do_ref, dq_ref, own_ref, far_ref, acc, s_sc, dp_sc, sl_sc, dpl_sc):
@@ -348,7 +474,7 @@
     hrecv,
 ):
     me, line, pos = place()
-    greet(line, pos, True)
+    greet(line, pos, (1, 3), False)
 
     def far(s):
         return pltpu.make_async_remote_copy(
@@ -488,37 +614,39 @@
 def shards(q, k, v, grad_mixed, out_weight, head_phase, segments_short, segments_long):
     me = lax.axis_index("seq")
     line, pos = me // RING, lax.rem(me, RING)
-    weight = lax.all_gather(out_weight, "fsdp", axis=0, tiled=True)
-
-    q_rows, kv_rows = pl.pallas_call(
-        send_qkv,
-        out_shape=(shaped(RING, ROWS, HS), shaped(2 * RING, 2, ROWS, HS)),
-        in_specs=[SM, VM, VM, VM],
-        out_specs=(VM, VM),
+    q_rows, kv_rows, do_rows = pl.pallas_call(
+        send_all,
+        out_shape=(
+            shaped(RING, ROWS, HS),
+            shaped(2 * RING, 2, ROWS, HS),
+            shaped(RING, ROWS, HS),
+        ),
+        in_specs=[SM, VM, VM, VM, VM, VM],
+        out_specs=(VM, VM, VM),
         scratch_shapes=[
             pltpu.VMEM((RING, 3, ROWS, HS), BF),
+            pltpu.VMEM((RING, ROWS, HS), BF),
+            pltpu.VMEM((HEADS, HS, grad_mixed.shape[2]), BF),
             DMA((2, RING)),
             DMA((2, RING)),
+            DMA((RING,)),
+            DMA((RING,)),
+            DMA((RING,)),
+            DMA((RING,)),
+            DMA,
+            DMA,
+            DMA((ROW_LINES,)),
+            DMA((ROW_LINES,)),
+            DMA((RING,)),
+            DMA((RING,)),
             DMA((RING,)),
             DMA((RING,)),
         ],
         compiler_params=pltpu.CompilerParams(
             collective_id=0, has_side_effects=True, vmem_limit_bytes=VMEM_LIMIT
         ),
-        name="send_qkv",
-    )(head_phase, q[0], k[0], v[0])
-
-    do_rows = pl.pallas_call(
-        send_grad,
-        out_shape=shaped(RING, ROWS, HS),
-        in_specs=[SM, VM, VM],
-        out_specs=VM,
-        scratch_shapes=[pltpu.VMEM((RING, ROWS, HS), BF), DMA((RING,)), DMA((RING,))],
-        compiler_params=pltpu.CompilerParams(
-            collective_id=1, has_side_effects=True, vmem_limit_bytes=VMEM_LIMIT
-        ),
-        name="send_grad",
-    )(head_phase, grad_mixed[0], weight)
+        name="send_all",
+    )(head_phase, q[0], k[0], v[0], grad_mixed[0], out_weight)
 
     origin = (line - 1) * (RING * TOK)
 
@@ -567,7 +695,7 @@
             DMA((RING,)),
         ],
         compiler_params=pltpu.CompilerParams(
-            collective_id=2, has_side_effects=True, vmem_limit_bytes=VMEM_LIMIT
+            collective_id=1, has_side_effects=True, vmem_limit_bytes=VMEM_LIMIT
         ),
         name="give_back",
     )(head_phase, dq_rows, own, far)

time: 248 us -> 155 us (0.62)
  the two profiles are of different devices: /device:TPU:107 before, /device:TPU:97 now
where the time goes in v2:
time: 155 us
  Pallas kernels  146 us (94%)
  local copies, waits for them, and re-layouts  4.36 us (3%)
  other arithmetic  4.08 us (3%)
    pallas_call x1, Pallas kernels, shards(): pl.pallas_call(give_back, out_shape=(shaped(TOK, HEADS * HS),) * 3, in_sp...  59.5 us
    pallas_call x1, Pallas kernels, shards(): pl.pallas_call(send_all, out_shape=(shaped(RING, ROWS, HS), shaped(2 * RI...  59.3 us
    pallas_call x1, Pallas kernels, shards(): pl.pallas_call(attend, out_shape=(shaped(RING, ROWS, HS), shaped(RING, 2,...  27.2 us
    unnamed x7, local copies, waits for them, and re-layouts  4.36 us

profile of v2, /device:TPU:97, one launch (start us, length us, event | category | flops | bytes accessed | tf_op | source)
XLA Modules:
  0.0 155.1 jit_solution(9830303180186272542)
XLA Ops:
  0.6 1.3 fusion
  1.9 0.8 select_reduce_fusion
  2.7 0.8 select_reduce_fusion.1
  3.5 1.2 pad_add_fusion.sc_ref
  4.7 59.3 %send_all.1 = (bf16[8,256,128]{2,1,0:T(8,128)(2,1)}, bf16[16,2,256,128]{3,2,1,0:T(8,128)(2,1)}, bf16[8,256,128]{2,1,0:T(8,128)(2,1)}) custom-call(s32[8]{0:T(128)} %phase_ref.3, bf16[512,1024]{1,0:T(8,128)(2,1)} %bitcast.13, bf16[512,1024]{1,0:T(8,128)(2,1)} %bitcast.14, bf16[512,1024]{1,0:T(8,128)(2,1)} %bitcast.15, bf16[512,2048]{1,0:T(8,128)(2,1)} %bitcast.9, ...), custom_call_target="tpu_custom_call" | custom-call | tf_op jit(solution)/shard_map/send_all/pallas_call | solution.py:617
  64.1 27.2 %attend.1 = (bf16[8,256,128]{2,1,0:T(8,128)(2,1)}, f32[8,2,256,128]{3,2,1,0:T(8,128)}, bf16[8,2,256,128]{3,2,1,0:T(8,128)(2,1)}) custom-call(s32[20]{0:T(128)} %pad_add_fusion.sc_ref, bf16[8,256,128]{2,1,0:T(8,128)(2,1)} %get-tuple-element.12.q_ref, bf16[16,2,256,128]{3,2,1,0:T(8,128)(2,1)} %get-tuple-element.13.kv_ref, ...), custom_call_target="tpu_custom_call" | custom-call | tf_op jit(solution)/shard_map/attend/pallas_call | solution.py:662
  91.2 59.5 %give_back.1 = (bf16[512,1024]{1,0:T(8,128)(2,1)}, bf16[512,1024]{1,0:T(8,128)(2,1)}, bf16[512,1024]{1,0:T(8,128)(2,1)}) custom-call(s32[8]{0:T(128)} %phase_ref.3, bf16[8,256,128]{2,1,0:T(8,128)(2,1)} %get-tuple-element.15.dq_ref, f32[8,2,256,128]{3,2,1,0:T(8,128)} %get-tuple-element.16.own_ref, bf16[8,2,256,128]{3,2,1,0:T(8,128)(2,1)} %get-tuple-element.17.far_ref), custom_call_target="tpu_custom_call" | custom-call | tf_op jit(solution)/shard_map/give_back/pallas_call | solution.py:682
  150.7 0.0 copy-start.1
  150.7 0.0 copy-start
  150.7 2.4 %copy.14 = bf16[1,512,1024]{2,1,0:T(8,128)(2,1)} copy(bf16[1,512,1024]{2,1,0:T(8,128)(2,1)} %bitcast.12) | data formatting | bytes 2097152
  153.1 0.0 copy-done.1
  153.1 1.0 copy.15
  154.1 0.0 copy-done
  154.1 1.0 copy.16
  (2 shorter events, 0.0 us)
Async XLA Ops:
  150.7 2.4 %copy-start.1 = (bf16[512,1024]{1,0:T(8,128)(2,1)S(1)}, bf16[512,1024]{1,0:T(8,128)(2,1)}, u32[]{:S(2)}) copy-start(bf16[512,1024]{1,0:T(8,128)(2,1)} %get-tuple-element.19) | copy-start | bytes 3145732
  150.7 3.4 %copy-start = (bf16[512,1024]{1,0:T(8,128)(2,1)S(1)}, bf16[512,1024]{1,0:T(8,128)(2,1)}, u32[]{:S(2)}) copy-start(bf16[512,1024]{1,0:T(8,128)(2,1)} %get-tuple-element.20) | copy-start | bytes 3145732

commit v3 on v2

--- a/solution.py
+++ b/solution.py
@@ -16,12 +16,16 @@
 RING = 8
 ROW_LINES = 4
 XS = 4
+PAIRS = 4
+NEAR = 5
+SHORT_TILES = RING * NEAR
+TILES = SHORT_TILES + 2 * PAIRS * PAIRS
 NEG = -1e30
 SCALE = 1.0 / math.sqrt(HS)
 NT = (((1,), (1,)), ((), ()))
 NN = (((1,), (0,)), ((), ()))
 TN = (((0,), (0,)), ((), ()))
-VMEM_LIMIT = 56 * 1024 * 1024
+VMEM_LIMIT = 60 * 1024 * 1024
 
 
 def dot(a, b, dims):
@@ -328,144 +332,32 @@
         to_core(j).wait_send()
 
 
-def attend(sc_ref, q_ref, kv_ref, do_ref, dq_ref, own_ref, far_ref, acc, s_sc, dp_sc, sl_sc, dpl_sc):
-    phase = sc_ref[0]
-    seq_start = sc_ref[1]
-    acc[...] = jnp.zeros_like(acc)
-
-    def low_of(tok, first, count):
-        low = jnp.full_like(tok, seq_start)
-        for n in range(count):
-            end = sc_ref[first + n]
-            low = jnp.where(tok >= end, jnp.maximum(low, end), low)
-        return low
-
-    def scalar_low(tok, first, count):
-        low = seq_start
-        for n in range(count):
-            end = sc_ref[first + n]
-            low = jnp.where(tok >= end, jnp.maximum(low, end), low)
-        return low
-
-    n_short, n_long = 15, 3
-    key_off = token_of(lax.broadcasted_iota(jnp.int32, (ROWS, 1), 0), phase)
-    lrow = lax.broadcasted_iota(jnp.int32, (4 * LROWS, 1), 0)
-    long_off = (lrow // LROWS) * TOK + 4 * (lrow & (LROWS - 1)) + phase
-    query_off = token_of(lax.broadcasted_iota(jnp.int32, (1, ROWS), 1), phase)
-
-    def block(i, _):
-        g = RING + i
-        q = q_ref[i]
-        do = do_ref[i]
-        ql, dol = q[:LROWS], do[:LROWS]
-        tok = g * TOK + query_off
-        tokl = tok[:, :LROWS]
-        low_s = low_of(tok, 2, n_short)
-        low_l = low_of(tokl, 2 + n_short, n_long)
-        first_s = scalar_low(g * TOK, 2, n_short) // TOK
-        first_l = scalar_low(g * TOK, 2 + n_short, n_long) // (4 * TOK)
-        first_s = jnp.maximum(first_s, g - 4)
-        last_l = g // 4 + 1
-
-        def long_kv(c, which):
-            return kv_ref[pl.ds(4 * c, 4), which, pl.ds(0, LROWS), :].reshape(4 * LROWS, HS)
-
-        def score(j, m):
-            s = dot(kv_ref[j, 0], q, NT)
-            u = j * TOK + key_off
-            s = jnp.where((u >= low_s) & (u <= tok), s, NEG)
-            s_sc[j - g + 4] = s
-            return jnp.maximum(m, jnp.max(s, axis=0, keepdims=True))
-
-        m = lax.fori_loop(first_s, g + 1, score, jnp.full((1, ROWS), NEG, jnp.float32))
-
-        def score_long(c, m):
-            s = dot(long_kv(c, 0), ql, NT)
-            u = c * (4 * TOK) + long_off
-            s = jnp.where((u >= low_l) & (u <= tokl), s, NEG)
-            sl_sc[c] = s
-            return jnp.maximum(m, jnp.max(s, axis=0, keepdims=True))
-
-        ml = lax.fori_loop(first_l, last_l, score_long, m[:, :LROWS])
-        m = jnp.concatenate([ml, m[:, LROWS:]], axis=1)
-
-        def weigh(j, carry):
-            l, d = carry
-            p = jnp.exp((s_sc[j - g + 4] - m) * SCALE)
-            dp = dot(kv_ref[j, 1], do, NT)
-            s_sc[j - g + 4] = p
-            dp_sc[j - g + 4] = dp
-            return (
-                l + jnp.sum(p, axis=0, keepdims=True),
-                d + jnp.sum(p * dp, axis=0, keepdims=True),
-            )
-
-        zero = jnp.zeros((1, ROWS), jnp.float32)
-        l, d = lax.fori_loop(first_s, g + 1, weigh, (zero, zero))
-
-        def weigh_long(c, carry):
-            l, d = carry
-            p = jnp.exp((sl_sc[c] - ml) * SCALE)
-            dp = dot(long_kv(c, 1), dol, NT)
-            sl_sc[c] = p
-            dpl_sc[c] = dp
-            return (
-                l + jnp.sum(p, axis=0, keepdims=True),
-                d + jnp.sum(p * dp, axis=0, keepdims=True),
-            )
-
-        ll, dl = lax.fori_loop(first_l, last_l, weigh_long, (l[:, :LROWS], d[:, :LROWS]))
-        l = jnp.concatenate([ll, l[:, LROWS:]], axis=1)
-        d = jnp.concatenate([dl, d[:, LROWS:]], axis=1)
-        inv = 1.0 / l
-        delta = d * inv
-        invl, deltal = inv[:, :LROWS], delta[:, :LROWS]
-
-        def back(j, dqt):
-            pr = s_sc[j - g + 4] * inv
-            ds = (pr * (dp_sc[j - g + 4] - delta)).astype(jnp.bfloat16)
-            acc[j, 1] += dot(pr.astype(jnp.bfloat16), do, NN)
-            acc[j, 0] += dot(ds, q, NN)
-            return dqt + dot(kv_ref[j, 0], ds, TN)
-
-        dqt = lax.fori_loop(first_s, g + 1, back, jnp.zeros((HS, ROWS), jnp.float32))
-
-        def back_long(c, dqt):
-            pr = sl_sc[c] * invl
-            ds = (pr * (dpl_sc[c] - deltal)).astype(jnp.bfloat16)
-            dv = dot(pr.astype(jnp.bfloat16), dol, NN)
-            dk = dot(ds, ql, NN)
-            acc[pl.ds(4 * c, 4), 1, pl.ds(0, LROWS), :] += dv.reshape(4, LROWS, HS)
-            acc[pl.ds(4 * c, 4), 0, pl.ds(0, LROWS), :] += dk.reshape(4, LROWS, HS)
-            return dqt + dot(long_kv(c, 0), ds, TN)
-
-        dqlt = lax.fori_loop(first_l, last_l, back_long, dqt[:, :LROWS])
-        dq_ref[i, pl.ds(0, LROWS), :] = (dqlt.T * SCALE).astype(jnp.bfloat16)
-        dq_ref[i, pl.ds(LROWS, LROWS), :] = (dqt[:, LROWS:].T * SCALE).astype(jnp.bfloat16)
-        return 0
-
-    lax.fori_loop(0, RING, block, 0)
-
-    def emit(b, _):
-        far_ref[b, 0] = (acc[b, 0] * SCALE).astype(jnp.bfloat16)
-        far_ref[b, 1] = acc[b, 1].astype(jnp.bfloat16)
-        own_ref[b, 0] = acc[RING + b, 0] * SCALE
-        own_ref[b, 1] = acc[RING + b, 1]
-        return 0
-
-    lax.fori_loop(0, RING, emit, 0)
-
-
-def give_back(
+def attend_back(
     phase_ref,
-    dq_ref,
-    own_ref,
-    far_ref,
+    short_ref,
+    long_ref,
+    q_ref,
+    kv_ref,
+    do_ref,
     gq_ref,
     gk_ref,
     gv_ref,
+    kt_ref,
+    lkv_ref,
+    lkt_ref,
+    lq_ref,
+    off_ref,
+    rows_ref,
+    p_ref,
+    dp_ref,
+    st_ref,
+    delta_ref,
+    acc,
+    dq_acc,
+    far_stage,
+    near,
+    dq_stage,
     stage,
-    near,
     got_q,
     got_kv,
     send_sem,
@@ -474,11 +366,14 @@
     hrecv,
 ):
     me, line, pos = place()
+    odd = lax.rem(line, 2)
     greet(line, pos, (1, 3), False)
+    phase = phase_ref[pos]
+    origin = (line - 1) * (RING * TOK)
 
     def far(s):
         return pltpu.make_async_remote_copy(
-            src_ref=far_ref.at[s],
+            src_ref=far_stage.at[s],
             dst_ref=near.at[s],
             send_sem=hsend.at[s],
             recv_sem=hrecv.at[s],
@@ -487,80 +382,299 @@
 
     def far_long(s):
         return pltpu.make_async_remote_copy(
-            src_ref=far_ref.at[s, :, pl.ds(0, LROWS)],
+            src_ref=far_stage.at[s, :, pl.ds(0, LROWS)],
             dst_ref=near.at[s, :, pl.ds(0, LROWS)],
             send_sem=hsend.at[s],
             recv_sem=hrecv.at[s],
             device_id={"seq": me - RING},
         )
 
-    def home(o, what):
-        s = lax.rem(pos + o, RING)
+    def home(s, what):
         if what == 0:
-            src, dst = dq_ref.at[s], got_q.at[pos]
+            src, dst = dq_stage.at[s], got_q.at[pos]
         else:
             src, dst = stage.at[s], got_kv.at[pos]
         return pltpu.make_async_remote_copy(
             src_ref=src,
             dst_ref=dst,
-            send_sem=send_sem.at[what, o],
-            recv_sem=recv_sem.at[what, o],
+            send_sem=send_sem.at[what, s],
+            recv_sem=recv_sem.at[what, pos],
             device_id={"seq": line * RING + s},
         )
 
-    def start_far(o, _):
-        s = lax.rem(pos + o, RING)
-
-        @pl.when((line > 0) & (s >= RING // 2))
-        def _():
-            far(s).start()
-
-        @pl.when((lax.rem(line, 2) == 1) & (s < RING // 2))
-        def _():
-            far_long(s).start()
-
-        return 0
-
-    lax.fori_loop(1, RING + 1, start_far, 0)
-
-    def start_q(o, _):
-        home(o, 0).start()
-        return 0
-
-    lax.fori_loop(1, RING, start_q, 0)
-    got_q[pos] = dq_ref[pos]
-
-    def start_kv(o, _):
-        s = lax.rem(pos + o, RING)
-        full = (line < ROW_LINES - 1) & (s >= RING // 2)
-        half = (lax.rem(line, 2) == 0) & (s < RING // 2)
-
-        @pl.when(full)
-        def _():
-            far(s).wait_recv()
-            stage[s] = (own_ref[s] + near[s].astype(jnp.float32)).astype(jnp.bfloat16)
-
-        @pl.when(half)
-        def _():
-            far_long(s).wait_recv()
-            stage[s, :, pl.ds(0, LROWS)] = (
-                own_ref[s, :, pl.ds(0, LROWS)] + near[s, :, pl.ds(0, LROWS)].astype(jnp.float32)
-            ).astype(jnp.bfloat16)
-            stage[s, :, pl.ds(LROWS, LROWS)] = own_ref[s, :, pl.ds(LROWS, LROWS)].astype(
+    def landed(s, what):
+        dst = got_q.at[s] if what == 0 else got_kv.at[s]
+        src = dq_stage.at[s] if what == 0 else stage.at[s]
+        return pltpu.make_async_remote_copy(
+            src_ref=src,
+            dst_ref=dst,
+            send_sem=send_sem.at[what, s],
+            recv_sem=recv_sem.at[what, s],
+            device_id={"seq": line * RING + lax.rem(pos + 1, RING)},
+        )
+
+    row = lax.broadcasted_iota(jnp.int32, (ROWS, LROWS), 0)
+    off_ref[0] = token_of(row, phase)
+    off_ref[1] = (row // LROWS) * TOK + 4 * (row & (LROWS - 1)) + phase
+
+    def low_of(tok, lengths, count):
+        low = jnp.full_like(tok, -origin)
+        end = -origin
+        for n in range(count):
+            end = end + lengths[n]
+            low = jnp.where(tok >= end, jnp.maximum(low, end), low)
+        return low
+
+    lane = lax.broadcasted_iota(jnp.int32, (1, ROWS), 1)
+    query_off = token_of(lane, phase)
+    pair_off = (lane // LROWS) * TOK + 4 * (lane & (LROWS - 1)) + phase
+
+    def prepare_query(i, _):
+        tok = (RING + i) * TOK + query_off
+        rows_ref[i, pl.ds(0, 1), :] = tok
+        rows_ref[i, pl.ds(1, 1), :] = low_of(tok, short_ref, 15)
+        return 0
+
+    lax.fori_loop(0, RING, prepare_query, 0)
+
+    def prepare_pair(ii, _):
+        tok = (RING + 2 * ii) * TOK + pair_off
+        rows_ref[RING + ii, pl.ds(0, 1), :] = tok
+        rows_ref[RING + ii, pl.ds(1, 1), :] = low_of(tok, long_ref, 3)
+        for e in range(2):
+            lq_ref[ii, 0, pl.ds(e * LROWS, LROWS), :] = q_ref[2 * ii + e, pl.ds(0, LROWS), :]
+            lq_ref[ii, 1, pl.ds(e * LROWS, LROWS), :] = do_ref[2 * ii + e, pl.ds(0, LROWS), :]
+        return 0
+
+    lax.fori_loop(0, PAIRS, prepare_pair, 0)
+
+    first_block = jnp.where(line > 0, RING // 2, RING)
+    first_pair = jnp.where(odd == 1, 0, PAIRS)
+
+    def prepare_key(g, _):
+        kt_ref[g] = kv_ref[g, 0].T
+        return 0
+
+    lax.fori_loop(first_block, 2 * RING, prepare_key, 0)
+
+    def prepare_key_pair(kp, _):
+        for e in range(2):
+            for w in range(2):
+                lkv_ref[kp, w, pl.ds(e * LROWS, LROWS), :] = kv_ref[
+                    2 * kp + e, w, pl.ds(0, LROWS), :
+                ]
+        lkt_ref[kp] = lkv_ref[kp, 0].T
+        return 0
+
+    lax.fori_loop(first_pair, 2 * PAIRS, prepare_key_pair, 0)
+
+    st_ref[:, pl.ds(0, 1), :] = jnp.full((TILES, 1, ROWS), NEG, jnp.float32)
+    st_ref[:, pl.ds(1, 3), :] = jnp.zeros((TILES, 3, ROWS), jnp.float32)
+    acc[...] = jnp.zeros_like(acc)
+    dq_acc[...] = jnp.zeros_like(dq_acc)
+
+    def tile(t, k, v, q, do, kind, tok, low):
+        off = off_ref[kind]
+        off = jnp.concatenate([off, off], axis=1)
+        s = dot(k, q, NT)
+        s = jnp.where((off >= low) & (off <= tok), s, NEG)
+        m = jnp.max(s, axis=0, keepdims=True)
+        p = jnp.exp((s - m) * SCALE)
+        dp = dot(v, do, NT)
+        p_ref[t] = p
+        dp_ref[t] = dp
+        st_ref[t, pl.ds(0, 1), :] = m
+        st_ref[t, pl.ds(1, 1), :] = jnp.sum(p, axis=0, keepdims=True)
+        st_ref[t, pl.ds(2, 1), :] = jnp.sum(p * dp, axis=0, keepdims=True)
+
+    def score_query(i, _):
+        tok = rows_ref[i, pl.ds(0, 1), :]
+        low = rows_ref[i, pl.ds(1, 1), :]
+
+        def one(g, _):
+            tile(
+                i * NEAR + RING + i - g,
+                kv_ref[g, 0],
+                kv_ref[g, 1],
+                q_ref[i],
+                do_ref[i],
+                0,
+                tok - g * TOK,
+                low - g * TOK,
+            )
+            return 0
+
+        lax.fori_loop(jnp.maximum(RING + i - (NEAR - 1), first_block), RING + i + 1, one, 0)
+        return 0
+
+    lax.fori_loop(0, RING, score_query, 0)
+
+    def score_pair(ii, _):
+        tok = rows_ref[RING + ii, pl.ds(0, 1), :]
+        low = rows_ref[RING + ii, pl.ds(1, 1), :]
+
+        def one(kp, _):
+            tile(
+                SHORT_TILES + ii * 2 * PAIRS + kp,
+                lkv_ref[kp, 0],
+                lkv_ref[kp, 1],
+                lq_ref[ii, 0],
+                lq_ref[ii, 1],
+                1,
+                tok - kp * (2 * TOK),
+                low - kp * (2 * TOK),
+            )
+            return 0
+
+        lax.fori_loop(first_pair, PAIRS + ii + 1, one, 0)
+        return 0
+
+    lax.fori_loop(0, PAIRS, score_pair, 0)
+
+    def join(ii, _):
+        base = SHORT_TILES + ii * 2 * PAIRS
+        lst = [st_ref[base + c] for c in range(2 * PAIRS)]
+        tops, invs, deltas = [], [], []
+        for e in range(2):
+            i = 2 * ii + e
+            sst = [st_ref[i * NEAR + c] for c in range(NEAR)]
+            here = slice(e * LROWS, (e + 1) * LROWS)
+            m = functools.reduce(jnp.maximum, [a[0:1] for a in sst])
+            ml = functools.reduce(jnp.maximum, [a[0:1, here] for a in lst], m[:, :LROWS])
+            m = jnp.concatenate([ml, m[:, LROWS:]], axis=1)
+            w = [jnp.exp((a[0:1] - m) * SCALE) for a in sst]
+            wl = [jnp.exp((a[0:1, here] - ml) * SCALE) for a in lst]
+            l = sum(x * a[1:2] for x, a in zip(w, sst))
+            d = sum(x * a[2:3] for x, a in zip(w, sst))
+            ll = sum((x * a[1:2, here] for x, a in zip(wl, lst)), l[:, :LROWS])
+            dl = sum((x * a[2:3, here] for x, a in zip(wl, lst)), d[:, :LROWS])
+            l = jnp.concatenate([ll, l[:, LROWS:]], axis=1)
+            d = jnp.concatenate([dl, d[:, LROWS:]], axis=1)
+            inv = 1.0 / l
+            delta_ref[i, pl.ds(0, 1), :] = d * inv
+            for c in range(NEAR):
+                st_ref[i * NEAR + c, pl.ds(3, 1), :] = w[c] * inv
+            tops.append(ml)
+            invs.append(inv[:, :LROWS])
+            deltas.append((d * inv)[:, :LROWS])
+        ml = jnp.concatenate(tops, axis=1)
+        il = jnp.concatenate(invs, axis=1)
+        delta_ref[RING + ii, pl.ds(0, 1), :] = jnp.concatenate(deltas, axis=1)
+        for c in range(2 * PAIRS):
+            st_ref[base + c, pl.ds(3, 1), :] = jnp.exp((lst[c][0:1] - ml) * SCALE) * il
+        return 0
+
+    lax.fori_loop(0, PAIRS, join, 0)
+
+    def back(t, q, do, kt, delta):
+        pr = p_ref[t] * st_ref[t, pl.ds(3, 1), :]
+        ds = (pr * (dp_ref[t] - delta)).astype(jnp.bfloat16)
+        return dot(ds, q, NN), dot(pr.astype(jnp.bfloat16), do, NN), dot(kt, ds, NN)
+
+    def back_pair(kp, first):
+        def one(ii, _):
+            dk, dv, dq = back(
+                SHORT_TILES + ii * 2 * PAIRS + kp,
+                lq_ref[ii, 0],
+                lq_ref[ii, 1],
+                lkt_ref[kp],
+                delta_ref[RING + ii, pl.ds(0, 1), :],
+            )
+            for e in range(2):
+                part = slice(e * LROWS, (e + 1) * LROWS)
+                acc[2 * kp + e, 0, pl.ds(0, LROWS), :] += dk[part]
+                acc[2 * kp + e, 1, pl.ds(0, LROWS), :] += dv[part]
+                dq_acc[2 * ii + e, :, pl.ds(0, LROWS)] += dq[:, part]
+            return 0
+
+        lax.fori_loop(first, PAIRS, one, 0)
+
+    def back_block(g, first, last):
+        def one(i, _):
+            dk, dv, dq = back(
+                i * NEAR + RING + i - g,
+                q_ref[i],
+                do_ref[i],
+                kt_ref[g],
+                delta_ref[i, pl.ds(0, 1), :],
+            )
+            acc[g, 0] += dk
+            acc[g, 1] += dv
+            dq_acc[i] += dq
+            return 0
+
+        lax.fori_loop(first, last, one, 0)
+
+    def far_pair(kp, _):
+        @pl.when(odd == 1)
+        def _():
+            back_pair(kp, 0)
+
+        for e in range(2):
+            g = 2 * kp + e
+
+            @pl.when(kp >= PAIRS // 2)
+            def _(g=g):
+                back_block(g, 0, g - (RING - NEAR))
+
+            far_stage[g, 0] = (acc[g, 0] * SCALE).astype(jnp.bfloat16)
+            far_stage[g, 1] = acc[g, 1].astype(jnp.bfloat16)
+
+            @pl.when(kp >= PAIRS // 2)
+            def _(g=g):
+                far(g).start()
+
+            @pl.when(kp < PAIRS // 2)
+            def _(g=g):
+                far_long(g).start()
+
+        return 0
+
+    first_far = jnp.where(odd == 1, 0, jnp.where(line > 0, PAIRS // 2, PAIRS))
+    lax.fori_loop(first_far, PAIRS, far_pair, 0)
+
+    def own_pair(kp, _):
+        back_pair(PAIRS + kp, kp)
+        for e in range(2):
+            b = 2 * kp + e
+            back_block(RING + b, b, jnp.minimum(b + NEAR, RING))
+            dq_stage[b] = (dq_acc[b].T * SCALE).astype(jnp.bfloat16)
+
+            @pl.when(b != pos)
+            def _(b=b):
+                home(b, 0).start()
+
+        for e in range(2):
+            b = 2 * kp + e
+            full = (line < ROW_LINES - 1) & (b >= RING // 2)
+            half = (odd == 0) & (b < RING // 2)
+
+            @pl.when(full)
+            def _(b=b):
+                far(b).wait_recv()
+
+            @pl.when(half)
+            def _(b=b):
+                far_long(b).wait_recv()
+                near[b, :, pl.ds(LROWS, LROWS)] = jnp.zeros((2, LROWS, HS), jnp.bfloat16)
+
+            @pl.when(jnp.logical_not(full | half))
+            def _(b=b):
+                near[b] = jnp.zeros((2, ROWS, HS), jnp.bfloat16)
+
+            stage[b, 0] = (acc[RING + b, 0] * SCALE + near[b, 0].astype(jnp.float32)).astype(
                 jnp.bfloat16
             )
-
-        @pl.when(jnp.logical_not(full | half))
-        def _():
-            stage[s] = own_ref[s].astype(jnp.bfloat16)
-
-        @pl.when(o < RING)
-        def _():
-            home(o, 1).start()
-
-        return 0
-
-    lax.fori_loop(1, RING + 1, start_kv, 0)
+            stage[b, 1] = (acc[RING + b, 1] + near[b, 1].astype(jnp.float32)).astype(jnp.bfloat16)
+
+            @pl.when(b != pos)
+            def _(b=b):
+                home(b, 1).start()
+
+        return 0
+
+    lax.fori_loop(0, PAIRS, own_pair, 0)
+    got_q[pos] = dq_stage[pos]
     got_kv[pos] = stage[pos]
 
     def unpack(o, _):
@@ -568,8 +682,8 @@
 
         @pl.when(o > 0)
         def _():
-            home(o, 0).wait_recv()
-            home(o, 1).wait_recv()
+            landed(h, 0).wait_recv()
+            landed(h, 1).wait_recv()
 
         spread = spread_matrix(phase_ref[h])
         cols = pl.ds(pl.multiple_of(h * HS, HS), HS)
@@ -581,8 +695,9 @@
     lax.fori_loop(0, RING, unpack, 0)
 
     def finish(o, _):
-        home(o, 0).wait_send()
-        home(o, 1).wait_send()
+        s = lax.rem(pos + o, RING)
+        home(s, 0).wait_send()
+        home(s, 1).wait_send()
         return 0
 
     lax.fori_loop(1, RING, finish, 0)
@@ -592,7 +707,7 @@
         def _():
             far(s).wait_send()
 
-        @pl.when((lax.rem(line, 2) == 1) & (s < RING // 2))
+        @pl.when((odd == 1) & (s < RING // 2))
         def _():
             far_long(s).wait_send()
 
@@ -648,44 +763,27 @@
         name="send_all",
     )(head_phase, q[0], k[0], v[0], grad_mixed[0], out_weight)
 
-    origin = (line - 1) * (RING * TOK)
-
-    def ends(lengths):
-        n = lengths.shape[0]
-        tri = jnp.arange(n)[None, :] <= jnp.arange(n)[:, None]
-        return jnp.sum(jnp.where(tri, lengths[None, :], 0), axis=1) - origin
-
-    phase_here = jnp.sum(jnp.where(jnp.arange(HEADS) == pos, head_phase, 0))
-    scalars = jnp.concatenate(
-        [jnp.stack([phase_here, -origin]), ends(segments_short), ends(segments_long)]
-    ).astype(jnp.int32)
-    dq_rows, own, far = pl.pallas_call(
-        attend,
-        out_shape=(
-            shaped(RING, ROWS, HS),
-            shaped(RING, 2, ROWS, HS, dtype=jnp.float32),
-            shaped(RING, 2, ROWS, HS),
-        ),
-        in_specs=[SM, VM, VM, VM],
-        out_specs=(VM, VM, VM),
-        scratch_shapes=[
-            pltpu.VMEM((2 * RING, 2, ROWS, HS), jnp.float32),
-            pltpu.VMEM((5, ROWS, ROWS), jnp.float32),
-            pltpu.VMEM((5, ROWS, ROWS), jnp.float32),
-            pltpu.VMEM((4, 4 * LROWS, LROWS), jnp.float32),
-            pltpu.VMEM((4, 4 * LROWS, LROWS), jnp.float32),
-        ],
-        compiler_params=pltpu.CompilerParams(vmem_limit_bytes=VMEM_LIMIT),
-        name="attend",
-    )(scalars, q_rows, kv_rows, do_rows)
-
     gq, gk, gv = pl.pallas_call(
-        give_back,
+        attend_back,
         out_shape=(shaped(TOK, HEADS * HS),) * 3,
-        in_specs=[SM, VM, VM, VM],
+        in_specs=[SM, SM, SM, VM, VM, VM],
         out_specs=(VM,) * 3,
         scratch_shapes=[
+            pltpu.VMEM((2 * RING, HS, ROWS), BF),
+            pltpu.VMEM((2 * PAIRS, 2, ROWS, HS), BF),
+            pltpu.VMEM((2 * PAIRS, HS, ROWS), BF),
+            pltpu.VMEM((PAIRS, 2, ROWS, HS), BF),
+            pltpu.VMEM((2, ROWS, LROWS), jnp.int32),
+            pltpu.VMEM((RING + PAIRS, 8, ROWS), jnp.int32),
+            pltpu.VMEM((TILES, ROWS, ROWS), jnp.float32),
+            pltpu.VMEM((TILES, ROWS, ROWS), jnp.float32),
+            pltpu.VMEM((TILES, 8, ROWS), jnp.float32),
+            pltpu.VMEM((RING + PAIRS, 8, ROWS), jnp.float32),
+            pltpu.VMEM((2 * RING, 2, ROWS, HS), jnp.float32),
+            pltpu.VMEM((RING, HS, ROWS), jnp.float32),
             pltpu.VMEM((RING, 2, ROWS, HS), BF),
+            pltpu.VMEM((RING, 2, ROWS, HS), BF),
+            pltpu.VMEM((RING, ROWS, HS), BF),
             pltpu.VMEM((RING, 2, ROWS, HS), BF),
             pltpu.VMEM((RING, ROWS, HS), BF),
             pltpu.VMEM((RING, 2, ROWS, HS), BF),
@@ -697,8 +795,8 @@
         compiler_params=pltpu.CompilerParams(
             collective_id=1, has_side_effects=True, vmem_limit_bytes=VMEM_LIMIT
         ),
-        name="give_back",
-    )(head_phase, dq_rows, own, far)
+        name="attend_back",
+    )(head_phase, segments_short, segments_long, q_rows, kv_rows, do_rows)
     return gq[None], gk[None], gv[None]
 
 

time: 155 us -> 146 us (0.942)
  the two profiles are of different devices: /device:TPU:97 before, /device:TPU:107 now
where the time goes in v3:
time: 146 us
  Pallas kernels  141 us (97%)
  local copies, waits for them, and re-layouts  4.36 us (3%)
    pallas_call x1, Pallas kernels, shards(): pl.pallas_call(attend_back, out_shape=(shaped(TOK, HEADS * HS),) * 3, in_...  81.6 us
    pallas_call x1, Pallas kernels, shards(): pl.pallas_call(send_all, out_shape=(shaped(RING, ROWS, HS), shaped(2 * RI...  59 us
    unnamed x7, local copies, waits for them, and re-layouts  4.36 us

profile of v3, /device:TPU:107, one launch (start us, length us, event | category | flops | bytes accessed | tf_op | source)
XLA Modules:
  0.0 145.7 jit_solution(3686045513000061180)
XLA Ops:
  0.6 59.0 %send_all.1 = (bf16[8,256,128]{2,1,0:T(8,128)(2,1)}, bf16[16,2,256,128]{3,2,1,0:T(8,128)(2,1)}, bf16[8,256,128]{2,1,0:T(8,128)(2,1)}) custom-call(s32[8]{0:T(128)} %phase_ref.3, bf16[512,1024]{1,0:T(8,128)(2,1)} %bitcast.11, bf16[512,1024]{1,0:T(8,128)(2,1)} %bitcast.12, bf16[512,1024]{1,0:T(8,128)(2,1)} %bitcast.13, bf16[512,2048]{1,0:T(8,128)(2,1)} %bitcast.7, ...), custom_call_target="tpu_custom_call" | custom-call | tf_op jit(solution)/shard_map/send_all/pallas_call | solution.py:732
  59.7 81.6 %attend_back.1 = (bf16[512,1024]{1,0:T(8,128)(2,1)}, bf16[512,1024]{1,0:T(8,128)(2,1)}, bf16[512,1024]{1,0:T(8,128)(2,1)}) custom-call(s32[8]{0:T(128)} %phase_ref.3, s32[15]{0:T(128)} %short_ref.1, s32[3]{0:T(128)} %long_ref.1, bf16[8,256,128]{2,1,0:T(8,128)(2,1)} %get-tuple-element.9.q_ref, bf16[16,2,256,128]{3,2,1,0:T(8,128)(2,1)} %get-tuple-element.10.kv_ref, ...), custom_call_target="tpu_custom_call" | custom-call | tf_op jit(solution)/shard_map/attend_back/pallas_call | solution.py:766
  141.3 0.0 copy-start.1
  141.3 0.0 copy-start
  141.3 2.4 %copy.14 = bf16[1,512,1024]{2,1,0:T(8,128)(2,1)} copy(bf16[1,512,1024]{2,1,0:T(8,128)(2,1)} %bitcast.10) | data formatting | bytes 2097152
  143.7 0.0 copy-done.1
  143.7 1.0 copy.15
  144.7 0.0 copy-done
  144.7 1.0 copy.16
Async XLA Ops:
  141.3 2.4 %copy-start.1 = (bf16[512,1024]{1,0:T(8,128)(2,1)S(1)}, bf16[512,1024]{1,0:T(8,128)(2,1)}, u32[]{:S(2)}) copy-start(bf16[512,1024]{1,0:T(8,128)(2,1)} %get-tuple-element.13) | copy-start | bytes 3145732
  141.3 3.4 %copy-start = (bf16[512,1024]{1,0:T(8,128)(2,1)S(1)}, bf16[512,1024]{1,0:T(8,128)(2,1)}, u32[]{:S(2)}) copy-start(bf16[512,1024]{1,0:T(8,128)(2,1)} %get-tuple-element.14) | copy-start | bytes 3145732

commit v4 on v3

v4 whole, which is shorter than its diff:
```python
import functools
import math

import jax
import jax.numpy as jnp
from jax import lax
from jax.experimental import pallas as pl
from jax.experimental.pallas import tpu as pltpu
from jax.sharding import PartitionSpec as P

HEADS = 8
HS = 128
TOK = 512
ROWS = 256
LROWS = 128
RING = 8
ROW_LINES = 4
XS = 4
PAIRS = 4
NEAR = 5
STATS = RING + PAIRS * PAIRS
NEG = -1e30
SCALE = 1.0 / math.sqrt(HS)
EXP_SCALE = SCALE * math.log2(math.e)
NT = (((1,), (1,)), ((), ()))
NN = (((1,), (0,)), ((), ()))
TN = (((0,), (0,)), ((), ()))
VMEM_LIMIT = 60 * 1024 * 1024


def dot(a, b, dims):
    return lax.dot_general(a, b, dims, preferred_element_type=jnp.float32)


def token_of(row, phase):
    other = jnp.where(phase < 2, phase + 2, phase - 2)
    return 4 * (row & (LROWS - 1)) + jnp.where(row < LROWS, phase, other)


def pick_matrix(phase):
    row = lax.broadcasted_iota(jnp.int32, (ROWS, TOK), 0)
    tok = lax.broadcasted_iota(jnp.int32, (ROWS, TOK), 1)
    return (tok == token_of(row, phase)).astype(jnp.float32).astype(jnp.bfloat16)


def spread_matrix(phase):
    row = lax.broadcasted_iota(jnp.int32, (TOK, ROWS), 1)
    tok = lax.broadcasted_iota(jnp.int32, (TOK, ROWS), 0)
    return (tok == token_of(row, phase)).astype(jnp.float32).astype(jnp.bfloat16)


def place():
    me = lax.axis_index("seq")
    return me, me // RING, lax.rem(me, RING)


def greet(line, pos, columns, gather):
    barrier = pltpu.get_barrier_semaphore()
    for o in range(1, RING):
        pl.semaphore_signal(
            barrier, inc=1, device_id={"seq": line * RING + lax.rem(pos + o, RING)}
        )
    for o in columns:
        pl.semaphore_signal(
            barrier, inc=1, device_id={"seq": lax.rem(line + o, ROW_LINES) * RING + pos}
        )
    total = RING - 1 + len(columns)
    if gather:
        f = lax.axis_index("fsdp")
        x, hi = f // 2, lax.rem(f, 2)
        pl.semaphore_signal(barrier, inc=1, device_id={"fsdp": 2 * x + 1 - hi})
        for o in range(1, XS):
            pl.semaphore_signal(barrier, inc=1, device_id={"fsdp": 2 * lax.rem(x + o, XS) + hi})
        total += XS
    pl.semaphore_wait(barrier, total)


def layer(
    phase_ref,
    short_ref,
    long_ref,
    q_ref,
    k_ref,
    v_ref,
    g_ref,
    w_ref,
    gq_ref,
    gk_ref,
    gv_ref,
    stage,
    gstage,
    w_all,
    qo_ref,
    kvo_ref,
    do_ref,
    kt_ref,
    lkv_ref,
    lkt_ref,
    lq_ref,
    off_ref,
    rows_ref,
    s_ref,
    p_ref,
    lp_ref,
    o_ref,
    lo_ref,
    st_ref,
    delta_ref,
    acc,
    dq_acc,
    far_stage,
    near,
    dq_stage,
    kv_stage,
    got_q,
    got_kv,
    send_sem,
    recv_sem,
    hsend,
    hrecv,
    gsend,
    grecv,
    zsend,
    zrecv,
    ysend,
    yrecv,
    xsend,
    xrecv,
    csend,
    crecv,
    bsend,
    brecv,
    fsend,
    frecv,
):
    me, line, pos = place()
    core = lax.rem(me, 2)
    f = lax.axis_index("fsdp")
    x, hi = f // 2, lax.rem(f, 2)
    mate = 2 * x + 1 - hi
    greet(line, pos, (1, 2, 3), True)
    half = pl.ds(pl.multiple_of(core * 64, 64), 64)
    piece = pl.ds(pl.multiple_of(core * 64 + line * 16, 16), 16)

    to_mate = pltpu.make_async_remote_copy(
        src_ref=w_ref.at[piece],
        dst_ref=w_all.at[f, piece],
        send_sem=zsend,
        recv_sem=zrecv,
        device_id={"fsdp": mate},
    )

    def along_y(o):
        return pltpu.make_async_remote_copy(
            src_ref=w_all.at[mate, piece],
            dst_ref=w_all.at[mate, piece],
            send_sem=ysend.at[o],
            recv_sem=yrecv.at[o],
            device_id={"seq": lax.rem(line + o, ROW_LINES) * RING + pos},
        )

    def along_x(j, own):
        m = jnp.maximum(j - 2, 0)
        src = w_ref.at[half] if own else w_all.at[mate, half]
        return pltpu.make_async_remote_copy(
            src_ref=src,
            dst_ref=w_all.at[f if own else mate, half],
            send_sem=xsend.at[j],
            recv_sem=xrecv.at[j],
            device_id={"fsdp": 2 * lax.rem(x + lax.rem(m, 3) + 1, XS) + hi},
        )

    def slot(j):
        m = jnp.maximum(j - 2, 0)
        other = 2 * lax.rem(x + XS - 1 - lax.rem(m, 3), XS) + jnp.where(m < 3, hi, 1 - hi)
        return jnp.where(j == 0, f, jnp.where(j == 1, mate, other))

    def to_core(j):
        return pltpu.make_async_remote_copy(
            src_ref=w_all.at[slot(j), half],
            dst_ref=w_all.at[slot(j), half],
            send_sem=csend.at[j],
            recv_sem=crecv.at[j],
            device_id={"seq": me + 1 - 2 * core},
        )

    to_mate.start()
    for j in range(2, 5):
        along_x(j, True).start()

    def packed(h):
        pick = pick_matrix(phase_ref[h])
        cols = pl.ds(pl.multiple_of(h * HS, HS), HS)
        return [dot(pick, ref[:, cols], NN).astype(jnp.bfloat16) for ref in (q_ref, k_ref, v_ref)]

    def to_peer(o, what):
        peer = line * RING + lax.rem(pos + o, RING)
        if what == 0:
            src, dst = stage.at[o, 0], qo_ref.at[pos]
        else:
            src, dst = stage.at[o, pl.ds(1, 2)], kvo_ref.at[RING + pos]
        return pltpu.make_async_remote_copy(
            src_ref=src,
            dst_ref=dst,
            send_sem=send_sem.at[what, o],
            recv_sem=recv_sem.at[what, o],
            device_id={"seq": peer},
        )

    def far(s):
        return pltpu.make_async_remote_copy(
            src_ref=kvo_ref.at[RING + s],
            dst_ref=kvo_ref.at[s],
            send_sem=hsend.at[s],
            recv_sem=hrecv.at[s],
            device_id={"seq": me + RING},
        )

    def far_long(s):
        return pltpu.make_async_remote_copy(
            src_ref=kvo_ref.at[RING + s, :, pl.ds(0, LROWS)],
            dst_ref=kvo_ref.at[s, :, pl.ds(0, LROWS)],
            send_sem=hsend.at[s],
            recv_sem=hrecv.at[s],
            device_id={"seq": me + RING},
        )

    def start(o, _):
        for i, rows in enumerate(packed(lax.rem(pos + o, RING))):
            stage[o, i] = rows
        to_peer(o, 1).start()
        to_peer(o, 0).start()
        return 0

    lax.fori_loop(1, RING, start, 0)

    to_mate.wait_recv()
    for o in range(1, ROW_LINES):
        along_y(o).start()
    own = packed(pos)
    qo_ref[pos] = own[0]
    kvo_ref[RING + pos, 0] = own[1]
    kvo_ref[RING + pos, 1] = own[2]
    w_all[f] = w_ref[...]
    for o in range(1, ROW_LINES):
        along_y(o).wait_recv()
    for j in range(5, 8):
        along_x(j, False).start()
    to_core(1).start()

    def to_head(j, h):
        return pltpu.make_async_remote_copy(
            src_ref=gstage.at[j],
            dst_ref=do_ref.at[pos],
            send_sem=gsend.at[j],
            recv_sem=grecv.at[pos],
            device_id={"seq": line * RING + h},
        )

    def grad_head(j, _):
        h = slot(j)

        @pl.when((j >= 1) & (j < RING - 1))
        def _():
            along_x(j + 1, True).wait_recv()
            to_core(j + 1).start()

        @pl.when(j >= 1)
        def _():
            to_core(j).wait_recv()

        full = dot(g_ref[...], w_all[h], NT).astype(jnp.bfloat16)
        rows = dot(pick_matrix(phase_ref[h]), full, NN).astype(jnp.bfloat16)

        @pl.when(h == pos)
        def _():
            do_ref[pos] = rows

        @pl.when(h != pos)
        def _():
            gstage[j] = rows
            to_head(j, h).start()

        return 0

    lax.fori_loop(0, RING, grad_head, 0)

    def forward(o, _):
        s = lax.rem(pos + RING - o, RING)

        @pl.when(o > 0)
        def _():
            to_peer(o, 1).wait_recv()

        @pl.when((line < ROW_LINES - 1) & (s >= RING // 2))
        def _():
            far(s).start()

        @pl.when((lax.rem(line, 2) == 0) & (s < RING // 2))
        def _():
            far_long(s).start()

        return 0

    lax.fori_loop(0, RING, forward, 0)


    phase = phase_ref[pos]
    odd = lax.rem(line, 2)
    origin = (line - 1) * (RING * TOK)
    row = lax.broadcasted_iota(jnp.int32, (ROWS, LROWS), 0)
    off_ref[0] = token_of(row, phase)
    off_ref[1] = (row // LROWS) * TOK + 4 * (row & (LROWS - 1)) + phase

    def low_of(tok, lengths, count):
        low = jnp.full_like(tok, -origin)
        end = -origin
        for n in range(count):
            end = end + lengths[n]
            low = jnp.where(tok >= end, jnp.maximum(low, end), low)
        return low

    lane = lax.broadcasted_iota(jnp.int32, (1, ROWS), 1)
    query_off = token_of(lane, phase)
    pair_off = (lane // LROWS) * TOK + 4 * (lane & (LROWS - 1)) + phase

    def prepare_query(i, _):
        tok = (RING + i) * TOK + query_off
        rows_ref[i, pl.ds(0, 1), :] = tok
        rows_ref[i, pl.ds(1, 1), :] = low_of(tok, short_ref, short_ref.shape[0])
        return 0

    lax.fori_loop(0, RING, prepare_query, 0)

    def prepare_pair(ii, _):
        tok = (RING + 2 * ii) * TOK + pair_off
        rows_ref[RING + ii, pl.ds(0, 1), :] = tok
        rows_ref[RING + ii, pl.ds(1, 1), :] = low_of(tok, long_ref, long_ref.shape[0])
        return 0

    lax.fori_loop(0, PAIRS, prepare_pair, 0)

    st_ref[:, pl.ds(0, 1), :] = jnp.full((STATS, 1, ROWS), NEG, jnp.float32)
    st_ref[:, pl.ds(1, 3), :] = jnp.zeros((STATS, 3, ROWS), jnp.float32)
    acc[...] = jnp.zeros_like(acc)
    dq_acc[...] = jnp.zeros_like(dq_acc)
    lo_ref[...] = jnp.zeros_like(lo_ref)

    @pl.when(line == 0)
    def _():
        kvo_ref[pl.ds(0, RING)] = jnp.zeros((RING, 2, ROWS, HS), jnp.bfloat16)

    def got_query(o, _):
        to_peer(o, 0).wait_recv()
        return 0

    lax.fori_loop(1, RING, got_query, 0)

    def prepare_key(g, _):
        kt_ref[g, 0] = kvo_ref[g, 0].T
        kt_ref[g, 1] = kvo_ref[g, 1].T
        return 0

    def prepare_key_pair(kp, _):
        for e in range(2):
            for w in range(2):
                lkv_ref[kp, w, pl.ds(e * LROWS, LROWS), :] = kvo_ref[
                    2 * kp + e, w, pl.ds(0, LROWS), :
                ]
        cols = pl.ds(pl.multiple_of(lax.rem(kp, 2) * ROWS, ROWS), ROWS)
        lkt_ref[kp // 2, 0, :, cols] = lkv_ref[kp, 0].T
        lkt_ref[kp // 2, 1, :, cols] = lkv_ref[kp, 1].T
        return 0

    def prepare_long_query(ii, _):
        for e in range(2):
            lq_ref[ii, 0, pl.ds(e * LROWS, LROWS), :] = qo_ref[2 * ii + e, pl.ds(0, LROWS), :]
        return 0

    lax.fori_loop(0, PAIRS, prepare_long_query, 0)
    lax.fori_loop(RING, 2 * RING, prepare_key, 0)
    lax.fori_loop(PAIRS, 2 * PAIRS, prepare_key_pair, 0)

    def strip(i, _):
        tok = rows_ref[i, pl.ds(0, 1), :]
        low = rows_ref[i, pl.ds(1, 1), :]
        q = qo_ref[i]
        off = jnp.concatenate([off_ref[0], off_ref[0]], axis=1)
        tops = []
        for d in range(NEAR):
            g = RING + i - d
            s = dot(kvo_ref[g, 0], q, NT)
            live = off >= low - g * TOK
            if d == 0:
                live = live & (off <= tok - g * TOK)
            s = jnp.where(live, s, NEG)
            s_ref[d] = s
            tops.append(jnp.max(s, axis=0, keepdims=True))
        m = functools.reduce(jnp.maximum, tops)
        l, o = jnp.zeros((1, ROWS), jnp.float32), jnp.zeros((HS, ROWS), jnp.float32)
        for d in range(NEAR):
            p = jnp.exp2((s_ref[d] - m) * EXP_SCALE)
            l = l + jnp.sum(p, axis=0, keepdims=True)
            w = p.astype(jnp.bfloat16)
            p_ref[i, d] = w
            o = o + dot(kt_ref[RING + i - d, 1], w, NN)
        st_ref[i, pl.ds(0, 1), :] = m
        st_ref[i, pl.ds(1, 1), :] = l
        o_ref[i] = o
        return 0

    def chunk(ii, c):
        tok = rows_ref[RING + ii, pl.ds(0, 1), :]
        low = rows_ref[RING + ii, pl.ds(1, 1), :]
        q = lq_ref[ii, 0]
        off = jnp.concatenate([off_ref[1], off_ref[1]], axis=1)
        scores = []
        for e in range(2):
            kp = 2 * c + e
            s = dot(lkv_ref[kp, 0], q, NT)
            at = kp * (2 * TOK)
            scores.append(jnp.where((off >= low - at) & (off <= tok - at), s, NEG))
        m = jnp.maximum(*[jnp.max(s, axis=0, keepdims=True) for s in scores])
        l = jnp.zeros((1, ROWS), jnp.float32)
        parts = []
        for e in range(2):
            p = jnp.exp2((scores[e] - m) * EXP_SCALE)
            l = l + jnp.sum(p, axis=0, keepdims=True)
            w = p.astype(jnp.bfloat16)
            lp_ref[ii, 2 * c + e] = w
            parts.append(w)
        t = RING + ii * PAIRS + c
        st_ref[t, pl.ds(0, 1), :] = m
        st_ref[t, pl.ds(1, 1), :] = l
        lo_ref[ii, c] = dot(lkt_ref[c, 1], jnp.concatenate(parts, axis=0), NN)

    def own_chunks(ii, _):
        chunk(ii, 2)

        @pl.when(ii >= 2)
        def _():
            chunk(ii, 3)

        return 0

    lax.fori_loop(0, PAIRS, own_chunks, 0)
    lax.fori_loop(RING // 2, RING, strip, 0)

    def got_far(s, _):
        @pl.when((line > 0) & (s >= RING // 2))
        def _():
            far(s).wait_recv()

        @pl.when((odd == 1) & (s < RING // 2))
        def _():
            far_long(s).wait_recv()

        return 0

    lax.fori_loop(0, RING, got_far, 0)
    lax.fori_loop(RING // 2, RING, prepare_key, 0)
    lax.fori_loop(0, RING // 2, strip, 0)

    @pl.when(odd == 1)
    def _():
        lax.fori_loop(0, PAIRS, prepare_key_pair, 0)

        def far_chunks(n, _):
            chunk(n // 2, lax.rem(n, 2))
            return 0

        lax.fori_loop(0, 2 * PAIRS, far_chunks, 0)

    def got_grad(j, _):
        @pl.when(j != pos)
        def _():
            pltpu.make_async_remote_copy(
                src_ref=gstage.at[j],
                dst_ref=do_ref.at[j],
                send_sem=gsend.at[j],
                recv_sem=grecv.at[j],
                device_id={"seq": line * RING + lax.rem(pos + 1, RING)},
            ).wait_recv()

        return 0

    lax.fori_loop(0, RING, got_grad, 0)

    def join(ii, _):
        base = RING + ii * PAIRS
        lst = [st_ref[base + c] for c in range(PAIRS)]
        tops, invs, deltas = [], [], []
        for e in range(2):
            i = 2 * ii + e
            lq_ref[ii, 1, pl.ds(e * LROWS, LROWS), :] = do_ref[i, pl.ds(0, LROWS), :]
            here = slice(e * LROWS, (e + 1) * LROWS)
            m = st_ref[i, pl.ds(0, 1), :]
            ml = functools.reduce(jnp.maximum, [a[0:1, here] for a in lst], m[:, :LROWS])
            w = jnp.exp2((m - jnp.concatenate([ml, m[:, LROWS:]], axis=1)) * EXP_SCALE)
            wl = [jnp.exp2((a[0:1, here] - ml) * EXP_SCALE) for a in lst]
            l = w * st_ref[i, pl.ds(1, 1), :]
            ll = sum((x * a[1:2, here] for x, a in zip(wl, lst)), l[:, :LROWS])
            inv = 1.0 / jnp.concatenate([ll, l[:, LROWS:]], axis=1)
            o = o_ref[i] * w
            ol = o[:, :LROWS]
            for c in range(PAIRS):
                ol = ol + lo_ref[ii, c, :, here] * wl[c]
            o = jnp.concatenate([ol, o[:, LROWS:]], axis=1)
            gt = do_ref[i].T.astype(jnp.float32)
            delta = jnp.sum(gt * (o * inv), axis=0, keepdims=True)
            delta_ref[i, pl.ds(0, 1), :] = delta
            st_ref[i, pl.ds(3, 1), :] = w * inv
            tops.append(ml)
            invs.append(inv[:, :LROWS])
            deltas.append(delta[:, :LROWS])
        ml = jnp.concatenate(tops, axis=1)
        il = jnp.concatenate(invs, axis=1)
        delta_ref[RING + ii, pl.ds(0, 1), :] = jnp.concatenate(deltas, axis=1)
        for c in range(PAIRS):
            st_ref[base + c, pl.ds(3, 1), :] = jnp.exp2((lst[c][0:1] - ml) * EXP_SCALE) * il
        return 0

    lax.fori_loop(0, PAIRS, join, 0)

    def back(p, t, v, q, do, kt, delta):
        pr = p.astype(jnp.float32) * st_ref[t, pl.ds(3, 1), :]
        dp = dot(v, do, NT)
        ds = (pr * (dp - delta)).astype(jnp.bfloat16)
        return dot(ds, q, NN), dot(pr.astype(jnp.bfloat16), do, NN), dot(kt, ds, NN)

    def back_pair(kp, first):
        cols = pl.ds(pl.multiple_of(lax.rem(kp, 2) * ROWS, ROWS), ROWS)

        def one(ii, _):
            dk, dv, dq = back(
                lp_ref[ii, kp],
                RING + ii * PAIRS + kp // 2,
                lkv_ref[kp, 1],
                lq_ref[ii, 0],
                lq_ref[ii, 1],
                lkt_ref[kp // 2, 0, :, cols],
                delta_ref[RING + ii, pl.ds(0, 1), :],
            )
            for e in range(2):
                part = slice(e * LROWS, (e + 1) * LROWS)
                acc[2 * kp + e, 0, pl.ds(0, LROWS), :] += dk[part]
                acc[2 * kp + e, 1, pl.ds(0, LROWS), :] += dv[part]
                dq_acc[2 * ii + e, :, pl.ds(0, LROWS)] += dq[:, part]
            return 0

        lax.fori_loop(first, PAIRS, one, 0)

    def back_block(g, first, last):
        def one(i, _):
            dk, dv, dq = back(
                p_ref[i, RING + i - g],
                i,
                kvo_ref[g, 1],
                qo_ref[i],
                do_ref[i],
                kt_ref[g, 0],
                delta_ref[i, pl.ds(0, 1), :],
            )
            acc[g, 0] += dk
            acc[g, 1] += dv
            dq_acc[i] += dq
            return 0

        lax.fori_loop(first, last, one, 0)

    def give(s):
        return pltpu.make_async_remote_copy(
            src_ref=far_stage.at[s],
            dst_ref=near.at[s],
            send_sem=fsend.at[s],
            recv_sem=frecv.at[s],
            device_id={"seq": me - RING},
        )

    def give_long(s):
        return pltpu.make_async_remote_copy(
            src_ref=far_stage.at[s, :, pl.ds(0, LROWS)],
            dst_ref=near.at[s, :, pl.ds(0, LROWS)],
            send_sem=fsend.at[s],
            recv_sem=frecv.at[s],
            device_id={"seq": me - RING},
        )

    def home(s, what):
        if what == 0:
            src, dst = dq_stage.at[s], got_q.at[pos]
        else:
            src, dst = kv_stage.at[s], got_kv.at[pos]
        return pltpu.make_async_remote_copy(
            src_ref=src,
            dst_ref=dst,
            send_sem=bsend.at[what, s],
            recv_sem=brecv.at[what, pos],
            device_id={"seq": line * RING + s},
        )

    def landed(s, what):
        dst = got_q.at[s] if what == 0 else got_kv.at[s]
        src = dq_stage.at[s] if what == 0 else kv_stage.at[s]
        return pltpu.make_async_remote_copy(
            src_ref=src,
            dst_ref=dst,
            send_sem=bsend.at[what, s],
            recv_sem=brecv.at[what, s],
            device_id={"seq": line * RING + lax.rem(pos + 1, RING)},
        )

    def far_pair(kp, _):
        @pl.when(odd == 1)
        def _():
            back_pair(kp, 0)

        for e in range(2):
            g = 2 * kp + e

            @pl.when(kp >= PAIRS // 2)
            def _(g=g):
                back_block(g, 0, g - (RING - NEAR))

            far_stage[g, 0] = (acc[g, 0] * SCALE).astype(jnp.bfloat16)
            far_stage[g, 1] = acc[g, 1].astype(jnp.bfloat16)

            @pl.when(kp >= PAIRS // 2)
            def _(g=g):
                give(g).start()

            @pl.when(kp < PAIRS // 2)
            def _(g=g):
                give_long(g).start()

        return 0

    first_far = jnp.where(odd == 1, 0, jnp.where(line > 0, PAIRS // 2, PAIRS))
    lax.fori_loop(first_far, PAIRS, far_pair, 0)

    def own_pair(kp, _):
        back_pair(PAIRS + kp, kp)
        for e in range(2):
            b = 2 * kp + e
            back_block(RING + b, b, jnp.minimum(b + NEAR, RING))
            dq_stage[b] = (dq_acc[b].T * SCALE).astype(jnp.bfloat16)

            @pl.when(b != pos)
            def _(b=b):
                home(b, 0).start()

        for e in range(2):
            b = 2 * kp + e
            full = (line < ROW_LINES - 1) & (b >= RING // 2)
            half = (odd == 0) & (b < RING // 2)

            @pl.when(full)
            def _(b=b):
                give(b).wait_recv()

            @pl.when(half)
            def _(b=b):
                give_long(b).wait_recv()
                near[b, :, pl.ds(LROWS, LROWS)] = jnp.zeros((2, LROWS, HS), jnp.bfloat16)

            @pl.when(jnp.logical_not(full | half))
            def _(b=b):
                near[b] = jnp.zeros((2, ROWS, HS), jnp.bfloat16)

            kv_stage[b, 0] = (acc[RING + b, 0] * SCALE + near[b, 0].astype(jnp.float32)).astype(
                jnp.bfloat16
            )
            kv_stage[b, 1] = (acc[RING + b, 1] + near[b, 1].astype(jnp.float32)).astype(jnp.bfloat16)

            @pl.when(b != pos)
            def _(b=b):
                home(b, 1).start()

        return 0

    lax.fori_loop(0, PAIRS, own_pair, 0)
    got_q[pos] = dq_stage[pos]
    got_kv[pos] = kv_stage[pos]

    def unpack(o, _):
        h = lax.rem(pos + RING - o, RING)

        @pl.when(o > 0)
        def _():
            landed(h, 0).wait_recv()
            landed(h, 1).wait_recv()

        spread = spread_matrix(phase_ref[h])
        cols = pl.ds(pl.multiple_of(h * HS, HS), HS)
        gq_ref[:, cols] = dot(spread, got_q[h], NN).astype(jnp.bfloat16)
        gk_ref[:, cols] = dot(spread, got_kv[h, 0], NN).astype(jnp.bfloat16)
        gv_ref[:, cols] = dot(spread, got_kv[h, 1], NN).astype(jnp.bfloat16)
        return 0

    lax.fori_loop(0, RING, unpack, 0)

    def finish(o, _):
        s = lax.rem(pos + o, RING)
        home(s, 0).wait_send()
        home(s, 1).wait_send()
        return 0

    lax.fori_loop(1, RING, finish, 0)

    def finish_far(s, _):
        @pl.when((line > 0) & (s >= RING // 2))
        def _():
            give(s).wait_send()

        @pl.when((odd == 1) & (s < RING // 2))
        def _():
            give_long(s).wait_send()

        return 0

    lax.fori_loop(0, RING, finish_far, 0)

    def sent(o, _):
        to_peer(o, 0).wait_send()
        to_peer(o, 1).wait_send()
        return 0

    lax.fori_loop(1, RING, sent, 0)

    def sent_grad(j, _):
        h = slot(j)

        @pl.when(h != pos)
        def _():
            to_head(j, h).wait_send()

        return 0

    lax.fori_loop(0, RING, sent_grad, 0)

    def sent_far(s, _):
        @pl.when((line < ROW_LINES - 1) & (s >= RING // 2))
        def _():
            far(s).wait_send()

        @pl.when((lax.rem(line, 2) == 0) & (s < RING // 2))
        def _():
            far_long(s).wait_send()

        return 0

    lax.fori_loop(0, RING, sent_far, 0)
    to_mate.wait_send()
    for o in range(1, ROW_LINES):
        along_y(o).wait_send()
    for j in range(2, 8):
        along_x(j, True).wait_send()
    for j in range(1, 8):
        to_core(j).wait_send()


VM = pl.BlockSpec(memory_space=pltpu.VMEM)
SM = pl.BlockSpec(memory_space=pltpu.SMEM)
DMA = pltpu.SemaphoreType.DMA
BF = jnp.bfloat16


def shaped(*dims, dtype=BF):
    return jax.ShapeDtypeStruct(dims, dtype)


def shards(q, k, v, grad_mixed, out_weight, head_phase, segments_short, segments_long):
    me = lax.axis_index("seq")
    line, pos = me // RING, lax.rem(me, RING)
    f32, i32 = jnp.float32, jnp.int32
    gq, gk, gv = pl.pallas_call(
        layer,
        out_shape=(shaped(TOK, HEADS * HS),) * 3,
        in_specs=[SM, SM, SM, VM, VM, VM, VM, VM],
        out_specs=(VM,) * 3,
        scratch_shapes=[
            pltpu.VMEM((RING, 3, ROWS, HS), BF),
            pltpu.VMEM((RING, ROWS, HS), BF),
            pltpu.VMEM((HEADS, HS, grad_mixed.shape[2]), BF),
            pltpu.VMEM((RING, ROWS, HS), BF),
            pltpu.VMEM((2 * RING, 2, ROWS, HS), BF),
            pltpu.VMEM((RING, ROWS, HS), BF),
            pltpu.VMEM((2 * RING, 2, HS, ROWS), BF),
            pltpu.VMEM((2 * PAIRS, 2, ROWS, HS), BF),
            pltpu.VMEM((PAIRS, 2, HS, 2 * ROWS), BF),
            pltpu.VMEM((PAIRS, 2, ROWS, HS), BF),
            pltpu.VMEM((2, ROWS, LROWS), i32),
            pltpu.VMEM((RING + PAIRS, 8, ROWS), i32),
            pltpu.VMEM((NEAR, ROWS, ROWS), f32),
            pltpu.VMEM((RING, NEAR, ROWS, ROWS), BF),
            pltpu.VMEM((PAIRS, 2 * PAIRS, ROWS, ROWS), BF),
            pltpu.VMEM((RING, HS, ROWS), f32),
            pltpu.VMEM((PAIRS, PAIRS, HS, ROWS), f32),
            pltpu.VMEM((STATS, 8, ROWS), f32),
            pltpu.VMEM((RING + PAIRS, 8, ROWS), f32),
            pltpu.VMEM((2 * RING, 2, ROWS, HS), f32),
            pltpu.VMEM((RING, HS, ROWS), f32),
            pltpu.VMEM((RING, 2, ROWS, HS), BF),
            pltpu.VMEM((RING, 2, ROWS, HS), BF),
            pltpu.VMEM((RING, ROWS, HS), BF),
            pltpu.VMEM((RING, 2, ROWS, HS), BF),
            pltpu.VMEM((RING, ROWS, HS), BF),
            pltpu.VMEM((RING, 2, ROWS, HS), BF),
            DMA((2, RING)),
            DMA((2, RING)),
            DMA((RING,)),
            DMA((RING,)),
            DMA((RING,)),
            DMA((RING,)),
            DMA,
            DMA,
            DMA((ROW_LINES,)),
            DMA((ROW_LINES,)),
            DMA((RING,)),
            DMA((RING,)),
            DMA((RING,)),
            DMA((RING,)),
            DMA((2, RING)),
            DMA((2, RING)),
            DMA((RING,)),
            DMA((RING,)),
        ],
        compiler_params=pltpu.CompilerParams(
            collective_id=0, has_side_effects=True, vmem_limit_bytes=VMEM_LIMIT
        ),
        name="layer",
    )(
        head_phase,
        segments_short,
        segments_long,
        q[0],
        k[0],
        v[0],
        grad_mixed[0],
        out_weight,
    )
    return gq[None], gk[None], gv[None]


def solution(mesh):
    placed = (
        P("fsdp", "seq", None),
        P("fsdp", "seq", None),
        P("fsdp", "seq", None),
        P("fsdp", "seq", None),
        P("fsdp", None),
        P(),
        P(),
        P(),
    )
    return jax.shard_map(
        shards,
        mesh=mesh,
        in_specs=placed,
        out_specs=(P("fsdp", "seq", None), P("fsdp", "seq", None), P("fsdp", "seq", None)),
        check_vma=False,
    )
```

time: 146 us -> 137 us (0.938)
  Pallas kernels: 141 us -> 132 us
    pallas_call x2 -> x1, Pallas kernels: 141 us -> 132 us  [shards(): pl.pallas_call(layer, out_shape=(shaped(TOK, HEADS * HS),) * 3, in_specs=...]
where the time goes in v4:
time: 137 us
  Pallas kernels  132 us (96%)
  local copies, waits for them, and re-layouts  4.36 us (3%)
    pallas_call x1, Pallas kernels, shards(): pl.pallas_call(layer, out_shape=(shaped(TOK, HEADS * HS),) * 3, in_specs=...  132 us
    unnamed x7, local copies, waits for them, and re-layouts  4.36 us

profile of v4, /device:TPU:107, one launch (start us, length us, event | category | flops | bytes accessed | tf_op | source)
XLA Modules:
  0.0 136.6 jit_solution(9454899656445298746)
XLA Ops:
  0.6 131.6 %layer.1 = (bf16[512,1024]{1,0:T(8,128)(2,1)}, bf16[512,1024]{1,0:T(8,128)(2,1)}, bf16[512,1024]{1,0:T(8,128)(2,1)}) custom-call(s32[8]{0:T(128)} %phase_ref.1, s32[15]{0:T(128)} %short_ref.1, s32[3]{0:T(128)} %long_ref.1, bf16[512,1024]{1,0:T(8,128)(2,1)} %bitcast.8, bf16[512,1024]{1,0:T(8,128)(2,1)} %bitcast.9, bf16[512,1024]{1,0:T(8,128)(2,1)} %bitcast.10, ...), custom_call_target="tpu_custom_call" | custom-call | tf_op jit(solution)/shard_map/layer/pallas_call | solution.py:776
  132.2 0.0 copy-start.1
  132.3 0.0 copy-start
  132.3 2.4 %copy.14 = bf16[1,512,1024]{2,1,0:T(8,128)(2,1)} copy(bf16[1,512,1024]{2,1,0:T(8,128)(2,1)} %bitcast.13) | data formatting | bytes 2097152
  134.7 0.0 copy-done.1
  134.7 1.0 copy.15
  135.6 0.0 copy-done
  135.7 1.0 copy.16
Async XLA Ops:
  132.2 2.4 %copy-start.1 = (bf16[512,1024]{1,0:T(8,128)(2,1)S(1)}, bf16[512,1024]{1,0:T(8,128)(2,1)}, u32[]{:S(2)}) copy-start(bf16[512,1024]{1,0:T(8,128)(2,1)} %get-tuple-element.7) | copy-start | bytes 3145732
  132.3 3.4 %copy-start = (bf16[512,1024]{1,0:T(8,128)(2,1)S(1)}, bf16[512,1024]{1,0:T(8,128)(2,1)}, u32[]{:S(2)}) copy-start(bf16[512,1024]{1,0:T(8,128)(2,1)} %get-tuple-element.8) | copy-start | bytes 3145732

commit v5 on v4

--- a/solution.py
+++ b/solution.py
@@ -229,10 +229,15 @@
         for i, rows in enumerate(packed(lax.rem(pos + o, RING))):
             stage[o, i] = rows
         to_peer(o, 1).start()
+        return 0
+
+    lax.fori_loop(1, RING, start, 0)
+
+    def start_query(o, _):
         to_peer(o, 0).start()
         return 0
 
-    lax.fori_loop(1, RING, start, 0)
+    lax.fori_loop(1, RING, start_query, 0)
 
     to_mate.wait_recv()
     for o in range(1, ROW_LINES):
@@ -522,51 +527,55 @@
 
     lax.fori_loop(0, PAIRS, join, 0)
 
-    def back(p, t, v, q, do, kt, delta):
-        pr = p.astype(jnp.float32) * st_ref[t, pl.ds(3, 1), :]
+    def back(weights, scales, deltas, v, kt, q, do):
         dp = dot(v, do, NT)
-        ds = (pr * (dp - delta)).astype(jnp.bfloat16)
-        return dot(ds, q, NN), dot(pr.astype(jnp.bfloat16), do, NN), dot(kt, ds, NN)
-
-    def back_pair(kp, first):
+        pbs, dss = [], []
+        for u, (w, a, delta) in enumerate(zip(weights, scales, deltas)):
+            pr = w.astype(jnp.float32) * a
+            dss.append((pr * (dp[:, u * ROWS : (u + 1) * ROWS] - delta)).astype(jnp.bfloat16))
+            pbs.append(pr.astype(jnp.bfloat16))
+        ds = jnp.concatenate(dss, axis=1)
+        pb = jnp.concatenate(pbs, axis=1)
+        return dot(ds, q, NN), dot(pb, do, NN), dot(kt, ds, NN)
+
+    def back_pair(kp, first, count):
         cols = pl.ds(pl.multiple_of(lax.rem(kp, 2) * ROWS, ROWS), ROWS)
-
-        def one(ii, _):
-            dk, dv, dq = back(
-                lp_ref[ii, kp],
-                RING + ii * PAIRS + kp // 2,
-                lkv_ref[kp, 1],
-                lq_ref[ii, 0],
-                lq_ref[ii, 1],
-                lkt_ref[kp // 2, 0, :, cols],
-                delta_ref[RING + ii, pl.ds(0, 1), :],
-            )
+        dk, dv, dq = back(
+            [lp_ref[first + u, kp] for u in range(count)],
+            [
+                st_ref[RING + (first + u) * PAIRS + kp // 2, pl.ds(3, 1), :]
+                for u in range(count)
+            ],
+            [delta_ref[RING + first + u, pl.ds(0, 1), :] for u in range(count)],
+            lkv_ref[kp, 1],
+            lkt_ref[kp // 2, 0, :, cols],
+            lq_ref[pl.ds(first, count), 0].reshape(count * ROWS, HS),
+            lq_ref[pl.ds(first, count), 1].reshape(count * ROWS, HS),
+        )
+        for e in range(2):
+            part = slice(e * LROWS, (e + 1) * LROWS)
+            acc[2 * kp + e, 0, pl.ds(0, LROWS), :] += dk[part]
+            acc[2 * kp + e, 1, pl.ds(0, LROWS), :] += dv[part]
+        for u in range(count):
             for e in range(2):
-                part = slice(e * LROWS, (e + 1) * LROWS)
-                acc[2 * kp + e, 0, pl.ds(0, LROWS), :] += dk[part]
-                acc[2 * kp + e, 1, pl.ds(0, LROWS), :] += dv[part]
-                dq_acc[2 * ii + e, :, pl.ds(0, LROWS)] += dq[:, part]
-            return 0
-
-        lax.fori_loop(first, PAIRS, one, 0)
-
-    def back_block(g, first, last):
-        def one(i, _):
-            dk, dv, dq = back(
-                p_ref[i, RING + i - g],
-                i,
-                kvo_ref[g, 1],
-                qo_ref[i],
-                do_ref[i],
-                kt_ref[g, 0],
-                delta_ref[i, pl.ds(0, 1), :],
-            )
-            acc[g, 0] += dk
-            acc[g, 1] += dv
-            dq_acc[i] += dq
-            return 0
-
-        lax.fori_loop(first, last, one, 0)
+                at = u * ROWS + e * LROWS
+                dq_acc[2 * (first + u) + e, :, pl.ds(0, LROWS)] += dq[:, at : at + LROWS]
+
+    def back_block(g, first, count):
+        d = RING + first - g
+        dk, dv, dq = back(
+            [p_ref[first + u, d + u] for u in range(count)],
+            [st_ref[first + u, pl.ds(3, 1), :] for u in range(count)],
+            [delta_ref[first + u, pl.ds(0, 1), :] for u in range(count)],
+            kvo_ref[g, 1],
+            kt_ref[g, 0],
+            qo_ref[pl.ds(first, count)].reshape(count * ROWS, HS),
+            do_ref[pl.ds(first, count)].reshape(count * ROWS, HS),
+        )
+        acc[g, 0] += dk
+        acc[g, 1] += dv
+        for u in range(count):
+            dq_acc[first + u] += dq[:, u * ROWS : (u + 1) * ROWS]
 
     def give(s):
         return pltpu.make_async_remote_copy(
@@ -610,75 +619,96 @@
             device_id={"seq": line * RING + lax.rem(pos + 1, RING)},
         )
 
-    def far_pair(kp, _):
-        @pl.when(odd == 1)
-        def _():
-            back_pair(kp, 0)
-
-        for e in range(2):
-            g = 2 * kp + e
-
-            @pl.when(kp >= PAIRS // 2)
-            def _(g=g):
-                back_block(g, 0, g - (RING - NEAR))
-
-            far_stage[g, 0] = (acc[g, 0] * SCALE).astype(jnp.bfloat16)
-            far_stage[g, 1] = acc[g, 1].astype(jnp.bfloat16)
-
-            @pl.when(kp >= PAIRS // 2)
-            def _(g=g):
-                give(g).start()
+    def emit_far(g):
+        far_stage[g, 0] = (acc[g, 0] * SCALE).astype(jnp.bfloat16)
+        far_stage[g, 1] = acc[g, 1].astype(jnp.bfloat16)
+
+    @pl.when(odd == 1)
+    def _():
+        def far_pair(kp, _):
+            back_pair(kp, 0, PAIRS)
 
             @pl.when(kp < PAIRS // 2)
-            def _(g=g):
-                give_long(g).start()
-
-        return 0
-
-    first_far = jnp.where(odd == 1, 0, jnp.where(line > 0, PAIRS // 2, PAIRS))
-    lax.fori_loop(first_far, PAIRS, far_pair, 0)
-
-    def own_pair(kp, _):
-        back_pair(PAIRS + kp, kp)
-        for e in range(2):
-            b = 2 * kp + e
-            back_block(RING + b, b, jnp.minimum(b + NEAR, RING))
-            dq_stage[b] = (dq_acc[b].T * SCALE).astype(jnp.bfloat16)
+            def _():
+                for e in range(2):
+                    emit_far(2 * kp + e)
+                    give_long(2 * kp + e).start()
+
+            return 0
+
+        lax.fori_loop(0, PAIRS, far_pair, 0)
+
+    @pl.when(line > 0)
+    def _():
+        for g in range(RING // 2, RING):
+            back_block(g, 0, g - (RING - NEAR))
+            emit_far(g)
+            give(g).start()
+
+    def joined(b):
+        full = (line < ROW_LINES - 1) & (b >= RING // 2)
+        half = (odd == 0) & (b < RING // 2)
+        return full, half
+
+    def own_block(b, count):
+        back_block(RING + b, b, count)
+        dq_stage[b] = (dq_acc[b].T * SCALE).astype(jnp.bfloat16)
+
+        @pl.when(b != pos)
+        def _():
+            home(b, 0).start()
+
+        full, half = joined(b)
+
+        @pl.when(jnp.logical_not(full | half))
+        def _():
+            kv_stage[b, 0] = (acc[RING + b, 0] * SCALE).astype(jnp.bfloat16)
+            kv_stage[b, 1] = acc[RING + b, 1].astype(jnp.bfloat16)
 
             @pl.when(b != pos)
-            def _(b=b):
-                home(b, 0).start()
-
-        for e in range(2):
-            b = 2 * kp + e
-            full = (line < ROW_LINES - 1) & (b >= RING // 2)
-            half = (odd == 0) & (b < RING // 2)
-
-            @pl.when(full)
-            def _(b=b):
-                give(b).wait_recv()
-
-            @pl.when(half)
-            def _(b=b):
-                give_long(b).wait_recv()
-                near[b, :, pl.ds(LROWS, LROWS)] = jnp.zeros((2, LROWS, HS), jnp.bfloat16)
-
-            @pl.when(jnp.logical_not(full | half))
-            def _(b=b):
-                near[b] = jnp.zeros((2, ROWS, HS), jnp.bfloat16)
-
+            def _():
+                home(b, 1).start()
+
+    def own_block_near(b, _):
+        own_block(b, NEAR)
+        return 0
+
+    for kp in range(PAIRS):
+        back_pair(PAIRS + kp, kp, PAIRS - kp)
+        if 2 * kp + NEAR < RING:
+            lax.fori_loop(2 * kp, 2 * kp + 2, own_block_near, 0)
+        else:
+            for e in range(2):
+                own_block(2 * kp + e, RING - 2 * kp - e)
+
+    def add_near(b, _):
+        full, half = joined(b)
+
+        @pl.when(full)
+        def _():
+            give(b).wait_recv()
+
+        @pl.when(half)
+        def _():
+            give_long(b).wait_recv()
+            near[b, :, pl.ds(LROWS, LROWS)] = jnp.zeros((2, LROWS, HS), jnp.bfloat16)
+
+        @pl.when(full | half)
+        def _():
             kv_stage[b, 0] = (acc[RING + b, 0] * SCALE + near[b, 0].astype(jnp.float32)).astype(
                 jnp.bfloat16
             )
-            kv_stage[b, 1] = (acc[RING + b, 1] + near[b, 1].astype(jnp.float32)).astype(jnp.bfloat16)
+            kv_stage[b, 1] = (acc[RING + b, 1] + near[b, 1].astype(jnp.float32)).astype(
+                jnp.bfloat16
+            )
 
             @pl.when(b != pos)
-            def _(b=b):
+            def _():
                 home(b, 1).start()
 
         return 0
 
-    lax.fori_loop(0, PAIRS, own_pair, 0)
+    lax.fori_loop(0, RING, add_near, 0)
     got_q[pos] = dq_stage[pos]
     got_kv[pos] = kv_stage[pos]
 

time: 137 us -> 124 us (0.905)
  Pallas kernels: 132 us -> 119 us
    pallas_call x1, Pallas kernels: 132 us -> 119 us  [shards(): pl.pallas_call(layer, out_shape=(shaped(TOK, HEADS * HS),) * 3, in_specs=...]
where the time goes in v5:
time: 124 us
  Pallas kernels  119 us (96%)
  local copies, waits for them, and re-layouts  4.36 us (4%)
    pallas_call x1, Pallas kernels, shards(): pl.pallas_call(layer, out_shape=(shaped(TOK, HEADS * HS),) * 3, in_specs=...  119 us
    unnamed x7, local copies, waits for them, and re-layouts  4.36 us

profile of v5, /device:TPU:107, one launch (start us, length us, event | category | flops | bytes accessed | tf_op | source)
XLA Modules:
  0.0 124.2 jit_solution(16033621423557227998)
XLA Ops:
  0.6 119.2 %layer.1 = (bf16[512,1024]{1,0:T(8,128)(2,1)}, bf16[512,1024]{1,0:T(8,128)(2,1)}, bf16[512,1024]{1,0:T(8,128)(2,1)}) custom-call(s32[8]{0:T(128)} %phase_ref.1, s32[15]{0:T(128)} %short_ref.1, s32[3]{0:T(128)} %long_ref.1, bf16[512,1024]{1,0:T(8,128)(2,1)} %bitcast.8, bf16[512,1024]{1,0:T(8,128)(2,1)} %bitcast.9, bf16[512,1024]{1,0:T(8,128)(2,1)} %bitcast.10, ...), custom_call_target="tpu_custom_call" | custom-call | tf_op jit(solution)/shard_map/layer/pallas_call | solution.py:806
  119.8 0.0 copy-start.1
  119.9 0.0 copy-start
  119.9 2.4 %copy.14 = bf16[1,512,1024]{2,1,0:T(8,128)(2,1)} copy(bf16[1,512,1024]{2,1,0:T(8,128)(2,1)} %bitcast.13) | data formatting | bytes 2097152
  122.3 0.0 copy-done.1
  122.3 1.0 copy.15
  123.2 0.0 copy-done
  123.2 1.0 copy.16
Async XLA Ops:
  119.8 2.4 %copy-start.1 = (bf16[512,1024]{1,0:T(8,128)(2,1)S(1)}, bf16[512,1024]{1,0:T(8,128)(2,1)}, u32[]{:S(2)}) copy-start(bf16[512,1024]{1,0:T(8,128)(2,1)} %get-tuple-element.7) | copy-start | bytes 3145732
  119.9 3.4 %copy-start = (bf16[512,1024]{1,0:T(8,128)(2,1)S(1)}, bf16[512,1024]{1,0:T(8,128)(2,1)}, u32[]{:S(2)}) copy-start(bf16[512,1024]{1,0:T(8,128)(2,1)} %get-tuple-element.8) | copy-start | bytes 3145732

commit v6 on v5

--- a/solution.py
+++ b/solution.py
@@ -159,20 +159,29 @@
             device_id={"seq": lax.rem(line + o, ROW_LINES) * RING + pos},
         )
 
-    def along_x(j, own):
-        m = jnp.maximum(j - 2, 0)
-        src = w_ref.at[half] if own else w_all.at[mate, half]
+    def along_x(step, kind, way):
+        hop = 1 if way == 0 else XS - 1
+        if step == 0:
+            at = f if kind == 0 else mate
+            rows = half
+            src = w_ref.at[half] if kind == 0 else w_all.at[mate, half]
+        else:
+            at = 2 * lax.rem(x + XS - hop, XS) + (hi if kind == 0 else 1 - hi)
+            rows = pl.ds(pl.multiple_of(core * 64 + way * 32, 32), 32)
+            src = w_all.at[at, rows]
         return pltpu.make_async_remote_copy(
             src_ref=src,
-            dst_ref=w_all.at[f if own else mate, half],
-            send_sem=xsend.at[j],
-            recv_sem=xrecv.at[j],
-            device_id={"fsdp": 2 * lax.rem(x + lax.rem(m, 3) + 1, XS) + hi},
+            dst_ref=w_all.at[at, rows],
+            send_sem=xsend.at[step, kind, way],
+            recv_sem=xrecv.at[step, kind, way],
+            device_id={"fsdp": 2 * lax.rem(x + hop, XS) + hi},
         )
 
     def slot(j):
         m = jnp.maximum(j - 2, 0)
-        other = 2 * lax.rem(x + XS - 1 - lax.rem(m, 3), XS) + jnp.where(m < 3, hi, 1 - hi)
+        r = lax.rem(m, 3)
+        hop = jnp.where(r == 0, XS - 1, r)
+        other = 2 * lax.rem(x + hop, XS) + jnp.where(m < 3, hi, 1 - hi)
         return jnp.where(j == 0, f, jnp.where(j == 1, mate, other))
 
     def to_core(j):
@@ -185,8 +194,19 @@
         )
 
     to_mate.start()
-    for j in range(2, 5):
-        along_x(j, True).start()
+    for way in range(2):
+        along_x(0, 0, way).start()
+
+    def pass_on(kind):
+        for way in range(2):
+            along_x(0, kind, way).wait_recv()
+            along_x(1, kind, way).start()
+            to_core(2 + 3 * kind + way).start()
+
+    def passed(kind):
+        for way in range(2):
+            along_x(1, kind, way).wait_recv()
+        to_core(4 + 3 * kind).start()
 
     def packed(h):
         pick = pick_matrix(phase_ref[h])
@@ -242,6 +262,7 @@
     to_mate.wait_recv()
     for o in range(1, ROW_LINES):
         along_y(o).start()
+    pass_on(0)
     own = packed(pos)
     qo_ref[pos] = own[0]
     kvo_ref[RING + pos, 0] = own[1]
@@ -249,8 +270,8 @@
     w_all[f] = w_ref[...]
     for o in range(1, ROW_LINES):
         along_y(o).wait_recv()
-    for j in range(5, 8):
-        along_x(j, False).start()
+    for way in range(2):
+        along_x(0, 1, way).start()
     to_core(1).start()
 
     def to_head(j, h):
@@ -265,10 +286,17 @@
     def grad_head(j, _):
         h = slot(j)
 
-        @pl.when((j >= 1) & (j < RING - 1))
-        def _():
-            along_x(j + 1, True).wait_recv()
-            to_core(j + 1).start()
+        @pl.when(j == 1)
+        def _():
+            passed(0)
+
+        @pl.when(j == 2)
+        def _():
+            pass_on(1)
+
+        @pl.when(j == 4)
+        def _():
+            passed(1)
 
         @pl.when(j >= 1)
         def _():
@@ -783,8 +811,10 @@
     to_mate.wait_send()
     for o in range(1, ROW_LINES):
         along_y(o).wait_send()
-    for j in range(2, 8):
-        along_x(j, True).wait_send()
+    for step in range(2):
+        for kind in range(2):
+            for way in range(2):
+                along_x(step, kind, way).wait_send()
     for j in range(1, 8):
         to_core(j).wait_send()
 
@@ -846,8 +876,8 @@
             DMA,
             DMA((ROW_LINES,)),
             DMA((ROW_LINES,)),
-            DMA((RING,)),
-            DMA((RING,)),
+            DMA((2, 2, 2)),
+            DMA((2, 2, 2)),
             DMA((RING,)),
             DMA((RING,)),
             DMA((2, RING)),

time: 124 us -> 124 us (level)
  no operation moved by 1% of the time
where the time goes in v6:
time: 124 us
  Pallas kernels  119 us (96%)
  local copies, waits for them, and re-layouts  4.36 us (4%)
    pallas_call x1, Pallas kernels, shards(): pl.pallas_call(layer, out_shape=(shaped(TOK, HEADS * HS),) * 3, in_specs=...  119 us
    unnamed x7, local copies, waits for them, and re-layouts  4.36 us

profile of v6, /device:TPU:107, one launch (start us, length us, event | category | flops | bytes accessed | tf_op | source)
XLA Modules:
  0.0 124.3 jit_solution(1991638952741568265)
XLA Ops:
  0.6 119.2 %layer.1 = (bf16[512,1024]{1,0:T(8,128)(2,1)}, bf16[512,1024]{1,0:T(8,128)(2,1)}, bf16[512,1024]{1,0:T(8,128)(2,1)}) custom-call(s32[8]{0:T(128)} %phase_ref.1, s32[15]{0:T(128)} %short_ref.1, s32[3]{0:T(128)} %long_ref.1, bf16[512,1024]{1,0:T(8,128)(2,1)} %bitcast.8, bf16[512,1024]{1,0:T(8,128)(2,1)} %bitcast.9, bf16[512,1024]{1,0:T(8,128)(2,1)} %bitcast.10, ...), custom_call_target="tpu_custom_call" | custom-call | tf_op jit(solution)/shard_map/layer/pallas_call | solution.py:836
  119.9 0.0 copy-start.1
  119.9 0.0 copy-start
  119.9 2.4 %copy.14 = bf16[1,512,1024]{2,1,0:T(8,128)(2,1)} copy(bf16[1,512,1024]{2,1,0:T(8,128)(2,1)} %bitcast.13) | data formatting | bytes 2097152
  122.3 0.0 copy-done.1
  122.3 1.0 copy.15
  123.3 0.0 copy-done
  123.3 1.0 copy.16
Async XLA Ops:
  119.9 2.4 %copy-start.1 = (bf16[512,1024]{1,0:T(8,128)(2,1)S(1)}, bf16[512,1024]{1,0:T(8,128)(2,1)}, u32[]{:S(2)}) copy-start(bf16[512,1024]{1,0:T(8,128)(2,1)} %get-tuple-element.7) | copy-start | bytes 3145732
  119.9 3.4 %copy-start = (bf16[512,1024]{1,0:T(8,128)(2,1)S(1)}, bf16[512,1024]{1,0:T(8,128)(2,1)}, u32[]{:S(2)}) copy-start(bf16[512,1024]{1,0:T(8,128)(2,1)} %get-tuple-element.8) | copy-start | bytes 3145732

commit v7 on v6

--- a/solution.py
+++ b/solution.py
@@ -84,9 +84,8 @@
     v_ref,
     g_ref,
     w_ref,
-    gq_ref,
-    gk_ref,
-    gv_ref,
+    got_q,
+    got_kv,
     stage,
     gstage,
     w_all,
@@ -112,8 +111,6 @@
     near,
     dq_stage,
     kv_stage,
-    got_q,
-    got_kv,
     send_sem,
     recv_sem,
     hsend,
@@ -257,7 +254,6 @@
         to_peer(o, 0).start()
         return 0
 
-    lax.fori_loop(1, RING, start_query, 0)
 
     to_mate.wait_recv()
     for o in range(1, ROW_LINES):
@@ -293,6 +289,7 @@
         @pl.when(j == 2)
         def _():
             pass_on(1)
+            lax.fori_loop(1, RING, start_query, 0)
 
         @pl.when(j == 4)
         def _():
@@ -312,11 +309,21 @@
         @pl.when(h != pos)
         def _():
             gstage[j] = rows
+
+        return 0
+
+    lax.fori_loop(0, RING, grad_head, 0)
+
+    def start_grad(j, _):
+        h = slot(j)
+
+        @pl.when(h != pos)
+        def _():
             to_head(j, h).start()
 
         return 0
 
-    lax.fori_loop(0, RING, grad_head, 0)
+    lax.fori_loop(0, RING, start_grad, 0)
 
     def forward(o, _):
         s = lax.rem(pos + RING - o, RING)
@@ -740,22 +747,13 @@
     got_q[pos] = dq_stage[pos]
     got_kv[pos] = kv_stage[pos]
 
-    def unpack(o, _):
+    def arrived(o, _):
         h = lax.rem(pos + RING - o, RING)
-
-        @pl.when(o > 0)
-        def _():
-            landed(h, 0).wait_recv()
-            landed(h, 1).wait_recv()
-
-        spread = spread_matrix(phase_ref[h])
-        cols = pl.ds(pl.multiple_of(h * HS, HS), HS)
-        gq_ref[:, cols] = dot(spread, got_q[h], NN).astype(jnp.bfloat16)
-        gk_ref[:, cols] = dot(spread, got_kv[h, 0], NN).astype(jnp.bfloat16)
-        gv_ref[:, cols] = dot(spread, got_kv[h, 1], NN).astype(jnp.bfloat16)
-        return 0
-
-    lax.fori_loop(0, RING, unpack, 0)
+        landed(h, 0).wait_recv()
+        landed(h, 1).wait_recv()
+        return 0
+
+    lax.fori_loop(1, RING, arrived, 0)
 
     def finish(o, _):
         s = lax.rem(pos + o, RING)
@@ -819,6 +817,13 @@
         to_core(j).wait_send()
 
 
+def spread(phase_ref, q_ref, kv_ref, gq_ref, gk_ref, gv_ref):
+    put = spread_matrix(phase_ref[pl.program_id(0)])
+    gq_ref[...] = dot(put, q_ref[0], NN).astype(jnp.bfloat16)
+    gk_ref[...] = dot(put, kv_ref[0, 0], NN).astype(jnp.bfloat16)
+    gv_ref[...] = dot(put, kv_ref[0, 1], NN).astype(jnp.bfloat16)
+
+
 VM = pl.BlockSpec(memory_space=pltpu.VMEM)
 SM = pl.BlockSpec(memory_space=pltpu.SMEM)
 DMA = pltpu.SemaphoreType.DMA
@@ -833,11 +838,11 @@
     me = lax.axis_index("seq")
     line, pos = me // RING, lax.rem(me, RING)
     f32, i32 = jnp.float32, jnp.int32
-    gq, gk, gv = pl.pallas_call(
+    got_q, got_kv = pl.pallas_call(
         layer,
-        out_shape=(shaped(TOK, HEADS * HS),) * 3,
+        out_shape=(shaped(RING, ROWS, HS), shaped(RING, 2, ROWS, HS)),
         in_specs=[SM, SM, SM, VM, VM, VM, VM, VM],
-        out_specs=(VM,) * 3,
+        out_specs=(VM, VM),
         scratch_shapes=[
             pltpu.VMEM((RING, 3, ROWS, HS), BF),
             pltpu.VMEM((RING, ROWS, HS), BF),
@@ -861,8 +866,6 @@
             pltpu.VMEM((2 * RING, 2, ROWS, HS), f32),
             pltpu.VMEM((RING, HS, ROWS), f32),
             pltpu.VMEM((RING, 2, ROWS, HS), BF),
-            pltpu.VMEM((RING, 2, ROWS, HS), BF),
-            pltpu.VMEM((RING, ROWS, HS), BF),
             pltpu.VMEM((RING, 2, ROWS, HS), BF),
             pltpu.VMEM((RING, ROWS, HS), BF),
             pltpu.VMEM((RING, 2, ROWS, HS), BF),
@@ -899,6 +902,19 @@
         grad_mixed[0],
         out_weight,
     )
+    block = pl.BlockSpec((TOK, HS), lambda h: (0, h))
+    gq, gk, gv = pl.pallas_call(
+        spread,
+        grid=(HEADS,),
+        out_shape=(shaped(TOK, HEADS * HS),) * 3,
+        in_specs=[
+            SM,
+            pl.BlockSpec((1, ROWS, HS), lambda h: (h, 0, 0)),
+            pl.BlockSpec((1, 2, ROWS, HS), lambda h: (h, 0, 0, 0)),
+        ],
+        out_specs=(block,) * 3,
+        name="spread",
+    )(head_phase, got_q, got_kv)
     return gq[None], gk[None], gv[None]
 
 

time: 124 us -> 125 us (level)
  Pallas kernels: 119 us -> 124 us
  local copies, waits for them, and re-layouts: 4.36 us -> 0 us
    pallas_call x1 -> x2, Pallas kernels: 119 us -> 124 us  [the longest x1 117 us: shards(): pl.pallas_call(layer, out_shape=(shaped(RING, ROWS, HS), shaped(RING, 2,...]
    unnamed x7 -> x0, local copies, waits for them, and re-layouts: 4.36 us -> none
where the time goes in v7:
time: 125 us
  Pallas kernels  124 us (99%)
    pallas_call x1, Pallas kernels, shards(): pl.pallas_call(layer, out_shape=(shaped(RING, ROWS, HS), shaped(RING, 2,...  117 us
    pallas_call x1, Pallas kernels, shards(): pl.pallas_call(spread, grid=(HEADS,), out_shape=(shaped(TOK, HEADS * HS),...  7.03 us

profile of v7, /device:TPU:107, one launch (start us, length us, event | category | flops | bytes accessed | tf_op | source)
XLA Modules:
  0.0 124.9 jit_solution(14857152998696514293)
XLA Ops:
  0.6 117.2 %layer.1 = (bf16[8,256,128]{2,1,0:T(8,128)(2,1)}, bf16[8,2,256,128]{3,2,1,0:T(8,128)(2,1)}) custom-call(s32[8]{0:T(128)} %phase_ref.3, s32[15]{0:T(128)} %short_ref.1, s32[3]{0:T(128)} %long_ref.1, bf16[512,1024]{1,0:T(8,128)(2,1)} %bitcast.8, bf16[512,1024]{1,0:T(8,128)(2,1)} %bitcast.9, bf16[512,1024]{1,0:T(8,128)(2,1)} %bitcast.10, ...), custom_call_target="tpu_custom_call" | custom-call | tf_op jit(solution)/shard_map/layer/pallas_call | solution.py:841
  117.9 7.0 %spread.1 = (bf16[512,1024]{1,0:T(8,128)(2,1)}, bf16[512,1024]{1,0:T(8,128)(2,1)}, bf16[512,1024]{1,0:T(8,128)(2,1)}) custom-call(s32[8]{0:T(128)} %phase_ref.3, bf16[8,256,128]{2,1,0:T(8,128)(2,1)} %get-tuple-element.8.q_ref, bf16[8,2,256,128]{3,2,1,0:T(8,128)(2,1)} %get-tuple-element.9.kv_ref), custom_call_target="tpu_custom_call" | custom-call | tf_op jit(solution)/shard_map/spread/pallas_call | solution.py:906

commit v8 on v7

--- a/solution.py
+++ b/solution.py
@@ -254,6 +254,7 @@
         to_peer(o, 0).start()
         return 0
 
+    lax.fori_loop(1, RING, start_query, 0)
 
     to_mate.wait_recv()
     for o in range(1, ROW_LINES):
@@ -289,7 +290,6 @@
         @pl.when(j == 2)
         def _():
             pass_on(1)
-            lax.fori_loop(1, RING, start_query, 0)
 
         @pl.when(j == 4)
         def _():
@@ -309,21 +309,11 @@
         @pl.when(h != pos)
         def _():
             gstage[j] = rows
+            to_head(j, h).start()
 
         return 0
 
     lax.fori_loop(0, RING, grad_head, 0)
-
-    def start_grad(j, _):
-        h = slot(j)
-
-        @pl.when(h != pos)
-        def _():
-            to_head(j, h).start()
-
-        return 0
-
-    lax.fori_loop(0, RING, start_grad, 0)
 
     def forward(o, _):
         s = lax.rem(pos + RING - o, RING)
@@ -389,12 +379,6 @@
     @pl.when(line == 0)
     def _():
         kvo_ref[pl.ds(0, RING)] = jnp.zeros((RING, 2, ROWS, HS), jnp.bfloat16)
-
-    def got_query(o, _):
-        to_peer(o, 0).wait_recv()
-        return 0
-
-    lax.fori_loop(1, RING, got_query, 0)
 
     def prepare_key(g, _):
         kt_ref[g, 0] = kvo_ref[g, 0].T
@@ -417,9 +401,16 @@
             lq_ref[ii, 0, pl.ds(e * LROWS, LROWS), :] = qo_ref[2 * ii + e, pl.ds(0, LROWS), :]
         return 0
 
-    lax.fori_loop(0, PAIRS, prepare_long_query, 0)
     lax.fori_loop(RING, 2 * RING, prepare_key, 0)
     lax.fori_loop(PAIRS, 2 * PAIRS, prepare_key_pair, 0)
+
+    def got_query(o, _):
+        to_peer(o, 0).wait_recv()
+        return 0
+
+    lax.fori_loop(1, RING, got_query, 0)
+
+    lax.fori_loop(0, PAIRS, prepare_long_query, 0)
 
     def strip(i, _):
         tok = rows_ref[i, pl.ds(0, 1), :]
@@ -818,10 +809,17 @@
 
 
 def spread(phase_ref, q_ref, kv_ref, gq_ref, gk_ref, gv_ref):
-    put = spread_matrix(phase_ref[pl.program_id(0)])
-    gq_ref[...] = dot(put, q_ref[0], NN).astype(jnp.bfloat16)
-    gk_ref[...] = dot(put, kv_ref[0, 0], NN).astype(jnp.bfloat16)
-    gv_ref[...] = dot(put, kv_ref[0, 1], NN).astype(jnp.bfloat16)
+    tok = lax.broadcasted_iota(jnp.int32, (TOK, ROWS), 0)
+    row = lax.broadcasted_iota(jnp.int32, (1, ROWS), 1)
+    for e in range(2):
+        of_row = token_of(row, phase_ref[2 * pl.program_id(0) + e])
+        put = jnp.where(tok == of_row, 1.0, 0.0).astype(jnp.bfloat16)
+        rows = jnp.concatenate([q_ref[e], kv_ref[e, 0], kv_ref[e, 1]], axis=1)
+        full = dot(put, rows, NN).astype(jnp.bfloat16)
+        here = pl.ds(e * HS, HS)
+        gq_ref[:, here] = full[:, :HS]
+        gk_ref[:, here] = full[:, HS : 2 * HS]
+        gv_ref[:, here] = full[:, 2 * HS :]
 
 
 VM = pl.BlockSpec(memory_space=pltpu.VMEM)
@@ -902,15 +900,15 @@
         grad_mixed[0],
         out_weight,
     )
-    block = pl.BlockSpec((TOK, HS), lambda h: (0, h))
+    block = pl.BlockSpec((TOK, 2 * HS), lambda h: (0, h))
     gq, gk, gv = pl.pallas_call(
         spread,
-        grid=(HEADS,),
+        grid=(HEADS // 2,),
         out_shape=(shaped(TOK, HEADS * HS),) * 3,
         in_specs=[
             SM,
-            pl.BlockSpec((1, ROWS, HS), lambda h: (h, 0, 0)),
-            pl.BlockSpec((1, 2, ROWS, HS), lambda h: (h, 0, 0, 0)),
+            pl.BlockSpec((2, ROWS, HS), lambda h: (h, 0, 0)),
+            pl.BlockSpec((2, 2, ROWS, HS), lambda h: (h, 0, 0, 0)),
         ],
         out_specs=(block,) * 3,
         name="spread",

time: 125 us -> 122 us (0.976)
  Pallas kernels: 124 us -> 121 us
    pallas_call x1, Pallas kernels: 7.03 us -> 4.73 us  [shards(): pl.pallas_call(spread, grid=(HEADS // 2,), out_shape=(shaped(TOK, HEADS *...]
where the time goes in v8:
time: 122 us
  Pallas kernels  121 us (99%)
    pallas_call x1, Pallas kernels, shards(): pl.pallas_call(layer, out_shape=(shaped(RING, ROWS, HS), shaped(RING, 2,...  116 us
    pallas_call x1, Pallas kernels, shards(): pl.pallas_call(spread, grid=(HEADS // 2,), out_shape=(shaped(TOK, HEADS *...  4.73 us

profile of v8, /device:TPU:107, one launch (start us, length us, event | category | flops | bytes accessed | tf_op | source)
XLA Modules:
  0.0 121.5 jit_solution(5666555269330166721)
XLA Ops:
  0.6 116.1 %layer.1 = (bf16[8,256,128]{2,1,0:T(8,128)(2,1)}, bf16[8,2,256,128]{3,2,1,0:T(8,128)(2,1)}) custom-call(s32[8]{0:T(128)} %phase_ref.3, s32[15]{0:T(128)} %short_ref.1, s32[3]{0:T(128)} %long_ref.1, bf16[512,1024]{1,0:T(8,128)(2,1)} %bitcast.8, bf16[512,1024]{1,0:T(8,128)(2,1)} %bitcast.9, bf16[512,1024]{1,0:T(8,128)(2,1)} %bitcast.10, ...), custom_call_target="tpu_custom_call" | custom-call | tf_op jit(solution)/shard_map/layer/pallas_call | solution.py:839
  116.8 4.7 %spread.1 = (bf16[512,1024]{1,0:T(8,128)(2,1)}, bf16[512,1024]{1,0:T(8,128)(2,1)}, bf16[512,1024]{1,0:T(8,128)(2,1)}) custom-call(s32[8]{0:T(128)} %phase_ref.3, bf16[8,256,128]{2,1,0:T(8,128)(2,1)} %get-tuple-element.8.q_ref, bf16[8,2,256,128]{3,2,1,0:T(8,128)(2,1)} %get-tuple-element.9.kv_ref), custom_call_target="tpu_custom_call" | custom-call | tf_op jit(solution)/shard_map/spread/pallas_call | solution.py:904
